TPU v7x, 128 devices: a whole 4x4x4 slice. The times are simulated.
128 devices in a mesh: dp: 8 (over y, z_lo), fsdp: 16 (over z_hi, x, core).
Axes of the slice: x: 4, y: 4, z: 4 (z_hi: 2, z_lo: 2; z = z_hi * 2 + z_lo), core: 2. Of those that a mesh axis runs over, the one named last changes fastest.
Arguments:
- tokens: bfloat16 [40960, 8192], P(('dp', 'fsdp')), may hold values from -6 to 6
- master: float32 [8192, 1024], P('fsdp'), may hold values from -0.0625 to 0.0625
- previous_down_factor: float32 [8192, 512], P('fsdp'), may hold values from -0.0625 to 0.0625
- previous_up_factor: float32 [512, 1024], P('fsdp'), may hold values from -0.25 to 0.25
- fresh_down: float32 [8192, 512], P('fsdp'), may hold values from -0.0625 to 0.0625
- fresh_up: float32 [512, 1024], P('fsdp'), may hold values from -0.25 to 0.25
- cotangent: bfloat16 [40960, 1024], P(('dp', 'fsdp')), may hold values from -6 to 6
Outputs:
- merged: float32 [8192, 1024], P('fsdp')
- values: bfloat16 [40960, 1024], P(('dp', 'fsdp'))
- input_gradient: bfloat16 [40960, 8192], P(('dp', 'fsdp'))
- down_factor_gradient: float32 [8192, 512], P('fsdp')
- up_factor_gradient: float32 [512, 1024], P('fsdp')
All inputs are finite; a program needn't handle non-finite values.
Results may differ from a plain program's by a relative error of at most 0.0051.
Values may be sent and summed in bfloat16 or wider, within the bound.
No kernel may reach another device: no remote copies, remote signals or barrier semaphores. Data moves between devices by JAX's collectives and lax.ppermute only.
A program may use at most 128 MiB of HBM per device.

v0:
```python
import jax
import jax.numpy as jnp
from jax import lax
from jax.sharding import PartitionSpec as P

adapter_scale = 0.25


def contract_trailing(left, right):
    return lax.dot_general(
        left, right, (((1,), (1,)), ((), ())), preferred_element_type=jnp.float32
    )


def contract_leading(left, right):
    return lax.dot_general(
        left, right, (((0,), (0,)), ((), ())), preferred_element_type=jnp.float32
    )


def shards(
    tokens, master, previous_down_factor, previous_up_factor, fresh_down, fresh_up, cotangent
):
    prior_whole = lax.all_gather(previous_up_factor, "fsdp", axis=0, tiled=True)
    merged = master + adapter_scale * jnp.dot(
        previous_down_factor,
        prior_whole,
        precision=lax.Precision.HIGHEST,
        preferred_element_type=jnp.float32,
    )
    weight_reduced_float = merged.astype(jnp.bfloat16)
    down_reduced_float = fresh_down.astype(jnp.bfloat16)
    up_reduced_float = fresh_up.astype(jnp.bfloat16)
    weight_wide_float, down_wide_float, up_wide_float = (
        lax.all_gather(weight_reduced_float, "fsdp", axis=0, tiled=True),
        lax.all_gather(down_reduced_float, "fsdp", axis=0, tiled=True),
        lax.all_gather(up_reduced_float, "fsdp", axis=0, tiled=True),
    )
    reduced_rank = jnp.dot(tokens, down_wide_float, preferred_element_type=jnp.float32).astype(
        jnp.bfloat16
    )
    values = (
        jnp.dot(tokens, weight_wide_float, preferred_element_type=jnp.float32)
        + adapter_scale * jnp.dot(reduced_rank, up_wide_float, preferred_element_type=jnp.float32)
    ).astype(jnp.bfloat16)
    backward_rank_rows = contract_trailing(cotangent, up_wide_float).astype(jnp.bfloat16)
    input_gradient = (
        contract_trailing(cotangent, weight_wide_float)
        + adapter_scale * contract_trailing(backward_rank_rows, down_wide_float)
    ).astype(jnp.bfloat16)
    feature_row_count = lax.all_to_all(tokens, "fsdp", split_axis=1, concat_axis=0, tiled=True)
    backward_total = lax.all_gather(backward_rank_rows, "fsdp", axis=0, tiled=True)
    down_piece_gradient = adapter_scale * contract_leading(feature_row_count, backward_total)
    owned_rows = previous_up_factor.shape[0]
    up_complete_factor = lax.psum(
        adapter_scale * contract_leading(reduced_rank, cotangent), ("dp", "fsdp")
    )
    up_factor_gradient = lax.dynamic_slice_in_dim(
        up_complete_factor, lax.axis_index("fsdp") * owned_rows, owned_rows, 0
    )
    down_factor_gradient = lax.psum(down_piece_gradient, "dp")
    return (merged, values, input_gradient, down_factor_gradient, up_factor_gradient)


def solution(mesh):
    in_specs = (
        P(("dp", "fsdp"), None),
        P("fsdp", None),
        P("fsdp", None),
        P("fsdp", None),
        P("fsdp", None),
        P("fsdp", None),
        P(("dp", "fsdp"), None),
    )
    out_specs = (
        P("fsdp", None),
        P(("dp", "fsdp"), None),
        P(("dp", "fsdp"), None),
        P("fsdp", None),
        P("fsdp", None),
    )
    return jax.shard_map(shards, mesh=mesh, in_specs=in_specs, out_specs=out_specs, check_vma=False)
```

profile of v0, /device:TPU:1, one launch (start us, length us, event | category | flops | bytes accessed | tf_op | source)
XLA Modules:
  0.0 667.5 jit_solution(2690450549280806141)
XLA Ops:
  7.2 1.6 convert_element_type.24
  8.9 50.9 %all-gather.12.cloned.1.call-done = bf16[512,1024]{1,0:T(8,128)(2,1)} async-done(((bf16[32,1024]{1,0:T(8,128)(2,1)}), bf16[512,1024]{1,0:T(8,128)(2,1)}) %all-gather.12.cloned.1.call-update) | async-done | bytes 1048592 | tf_op jit(solution)/shard_map/all_gather | solution.py:37
  59.8 2.7 convolution_convert_fusion.1
  62.6 2.1 convert_element_type.22
  64.7 5.4 copy.20
  70.1 4.6 all-to-all-start
  75.3 76.8 %all-to-all-done = bf16[320,16,512]{2,0,1:T(8,128)(2,1)} async-done(((bf16[320,16,512]{2,0,1:T(8,128)(2,1)}), bf16[320,16,512]{2,0,1:T(8,128)(2,1)}, u32[]{:S(2)}, u32[]{:S(2)}) %all-to-all-start) | async-done | bytes 5242912 | tf_op jit(solution)/shard_map/all_to_all | solution.py:51
  152.1 7.5 %all-gather.14.cloned.1.call-done = bf16[5120,512]{1,0:T(8,128)(2,1)} async-done(((bf16[320,512]{1,0:T(8,128)(2,1)}), bf16[5120,512]{1,0:T(8,128)(2,1)}) %all-gather.14.cloned.1.call-update) | async-done | bytes 5242896 | tf_op jit(solution)/shard_map/all_gather | solution.py:52
  159.5 7.9 %fusion.3 = f32[512,512]{0,1:T(8,128)} fusion(bf16[5120,512]{1,0:T(8,128)(2,1)} %all-gather.14.cloned.1.call-done, bf16[5120,512]{1,0:T(8,128)(2,1)} %bitcast.3), kind=kOutput, calls=%fused_computation.11 | convolution fusion | flops 2684616704 | bytes 11534336 | tf_op jit(solution)/shard_map/dot_general | solution.py:16
  167.5 67.3 %all-gather.10.cloned.1.call-done = bf16[8192,512]{1,0:T(8,128)(2,1)} async-done(((bf16[512,512]{1,0:T(8,128)(2,1)}), bf16[8192,512]{1,0:T(8,128)(2,1)}) %all-gather.10.cloned.1.call-update) | async-done | bytes 8388624 | tf_op jit(solution)/shard_map/all_gather | solution.py:36
  234.8 7.8 %convolution_convert_fusion = bf16[320,512]{1,0:T(8,128)(2,1)S(1)} fusion(bf16[320,8192]{1,0:T(8,128)(2,1)} %param.7, bf16[8192,512]{1,0:T(8,128)(2,1)} %all-gather.10.cloned.1.call-done), kind=kOutput, calls=%fused_computation.13 | convolution fusion | flops 2684518400 | bytes 13959168 | tf_op jit(solution)/shard_map/dot_general | solution.py:39
  242.6 0.7 copy-done.4
  243.3 3.3 convolution_multiply_fusion.1
  246.9 36.3 %all-gather.6.cloned.1.call-done = f32[512,1024]{1,0:T(8,128)} async-done(((f32[32,1024]{1,0:T(8,128)}), f32[512,1024]{1,0:T(8,128)}) %all-gather.6.cloned.1.call-update) | async-done | bytes 2097168 | tf_op jit(solution)/shard_map/all_gather | solution.py:24
  283.2 6.9 %fusion.5 = (bf16[512,1024]{1,0:T(8,128)(2,1)}, f32[512,1024]{1,0:T(8,128)}) fusion(f32[512,1024]{1,0:T(8,128)S(1)} %copy-done.2, f32[512,512]{1,0:T(8,128)S(1)} %copy-done, f32[512,1024]{1,0:T(8,128)} %all-gather.6.cloned.1.call-done), kind=kOutput, calls=%fused_computation.16 | convolution fusion | flops 3222798336 | bytes 8388608 | tf_op jit(solution)/shard_map/dot_general | solution.py:25
  290.1 68.0 %all-reduce.3.cloned.1.call-done = f32[512,512]{0,1:T(8,128)} async-done(((f32[512,512]{0,1:T(8,128)}), f32[512,512]{0,1:T(8,128)}) %all-reduce.3.cloned.1.call-update) | async-done | bytes 1048592 | tf_op jit(solution)/shard_map/psum | solution.py:61
  358.1 2.5 copy.17
  360.6 1.8 convolution_multiply_fusion.2
  362.5 11.6 %convolution_multiply_fusion = f32[320,8192]{1,0:T(8,128)} fusion(bf16[320,512]{1,0:T(8,128)(2,1)S(1)} %copy-done.3, bf16[8192,512]{1,0:T(8,128)(2,1)} %all-gather.10.cloned.1.call-done), kind=kOutput, calls=%fused_computation | convolution fusion | flops 2686976000 | bytes 19202048 | tf_op jit(solution)/shard_map/dot_general | solution.py:10
  374.1 143.4 %all-reduce.5.cloned.1.call-done = f32[512,1024]{1,0:T(8,128)} async-done(((f32[512,1024]{1,0:T(8,128)}), f32[512,1024]{1,0:T(8,128)}) %all-reduce.5.cloned.1.call-update) | async-done | bytes 2097168 | tf_op jit(solution)/shard_map/psum | solution.py:55
  517.5 1.6 constant_dynamic-slice_fusion
  519.1 109.9 %all-gather.8.cloned.1.call-done = bf16[8192,1024]{1,0:T(8,128)(2,1)} async-done(((bf16[512,1024]{1,0:T(8,128)(2,1)}), bf16[8192,1024]{1,0:T(8,128)(2,1)}) %all-gather.8.cloned.1.call-update) | async-done | bytes 16777232 | tf_op jit(solution)/shard_map/all_gather | solution.py:35
  629.0 20.2 %fusion.1 = bf16[320,8192]{1,0:T(8,128)(2,1)} fusion(f32[320,8192]{1,0:T(8,128)} %convolution_multiply_fusion, bf16[8192,1024]{1,0:T(8,128)(2,1)} %all-gather.8.cloned.1.call-done, bf16[320,1024]{1,0:T(8,128)(2,1)S(1)} %copy-done.5), kind=kOutput, calls=%fused_computation.3 | convolution fusion | flops 5373952000 | bytes 33161216 | tf_op jit(solution)/shard_map/dot_general | solution.py:10
  649.2 11.4 %fusion.4 = bf16[320,1024]{1,0:T(8,128)(2,1)} fusion(f32[320,1024]{1,0:T(8,128)S(1)} %convolution_multiply_fusion.2, bf16[320,8192]{1,0:T(8,128)(2,1)} %param.7, bf16[8192,1024]{1,0:T(8,128)(2,1)} %all-gather.8.cloned.1.call-done), kind=kOutput, calls=%fused_computation.12 | convolution fusion | flops 5369364480 | bytes 23986176 | tf_op jit(solution)/shard_map/dot_general | solution.py:43
  (25 shorter events, 1.1 us)
Async XLA Ops:
  7.2 276.1 %copy-start = (f32[512,512]{1,0:T(8,128)S(1)}, f32[512,512]{1,0:T(8,128)}, u32[]{:S(2)}) copy-start(f32[512,512]{1,0:T(8,128)} %param.9) | copy-start | bytes 3145732
  7.2 52.6 %all-gather.12.cloned.1.call-start = ((), (), s32[]{:S(2)}) async-start(), calls=%async_computation.4 | async-start | bytes 1114112 | tf_op jit(solution)/shard_map/all_gather | solution.py:37
  8.9 150.7 %all-gather.14.cloned.1.call-start = ((), (), s32[]{:S(2)}) async-start(), calls=%async_computation.5 | async-start | bytes 5570560 | tf_op jit(solution)/shard_map/all_gather | solution.py:52
  62.5 172.3 %all-gather.10.cloned.1.call-start = ((), (), s32[]{:S(2)}) async-start(), calls=%async_computation.3 | async-start | bytes 8912896 | tf_op jit(solution)/shard_map/all_gather | solution.py:36
  70.1 82.0 %all-to-all-start = ((bf16[320,16,512]{2,0,1:T(8,128)(2,1)}), bf16[320,16,512]{2,0,1:T(8,128)(2,1)}, u32[]{:S(2)}, u32[]{:S(2)}) async-start(bf16[320,16,512]{2,0,1:T(8,128)(2,1)} %bitcast.39), calls=%async_computation | async-start | bytes 10485760 | tf_op jit(solution)/shard_map/all_to_all | solution.py:51
  74.7 208.5 %all-gather.6.cloned.1.call-start = ((), (), s32[]{:S(2)}) async-start(), calls=%async_computation.1 | async-start | bytes 2228224 | tf_op jit(solution)/shard_map/all_gather | solution.py:24
  75.3 282.9 %all-reduce.3.cloned.1.call-start = ((), (), s32[]{:S(2)}) async-start(), calls=%async_computation.6 | async-start | bytes 2097152 | tf_op jit(solution)/shard_map/psum | solution.py:61
  167.5 350.1 %all-reduce.5.cloned.1.call-start = ((), (), s32[]{:S(2)}) async-start(), calls=%async_computation.7 | async-start | bytes 4194304 | tf_op jit(solution)/shard_map/psum | solution.py:55
  242.6 0.7 copy-start.4
  243.3 39.9 %copy-start.2 = (f32[512,1024]{1,0:T(8,128)S(1)}, f32[512,1024]{1,0:T(8,128)}, u32[]{:S(2)}) copy-start(f32[512,1024]{1,0:T(8,128)} %param.8) | copy-start | bytes 6291460
  246.7 115.8 %copy-start.3 = (bf16[320,512]{1,0:T(8,128)(2,1)S(1)}, bf16[320,512]{1,0:T(8,128)(2,1)}, u32[]{:S(2)}) copy-start(bf16[320,512]{1,0:T(8,128)(2,1)} %convolution_convert_fusion.1) | copy-start | bytes 983044
  246.7 382.3 %all-gather.8.cloned.1.call-start = ((), (), s32[]{:S(2)}) async-start(), calls=%async_computation.2 | async-start | bytes 17825792 | tf_op jit(solution)/shard_map/all_gather | solution.py:35
  362.5 266.5 %copy-start.5 = (bf16[320,1024]{1,0:T(8,128)(2,1)S(1)}, bf16[320,1024]{1,0:T(8,128)(2,1)}, u32[]{:S(2)}) copy-start(bf16[320,1024]{1,0:T(8,128)(2,1)} %param.13) | copy-start | bytes 1966084
  649.2 11.4 %copy-start.1 = (f32[512,512]{1,0:T(8,128)S(1)}, f32[512,512]{1,0:T(8,128)}, u32[]{:S(2)}) copy-start(f32[512,512]{1,0:T(8,128)} %param.9) | copy-start | bytes 3145732
Sparse Core Ops, SparseCore 0:
  11.0 48.7 all-gather.11
  62.6 96.8 all-gather.13
  162.6 72.1 all-gather.9
  237.1 46.0 all-gather.5
  286.1 71.9 all-reduce.2
  363.4 154.0 all-reduce.4
  520.0 109.0 all-gather.7
where the time goes:
time: 668 us
  waiting for transfers between devices  561 us (84%)
  matrix products  73.7 us (11%)
  between operations  14.2 us (2%)
  local copies, waits for them, and re-layouts  10.3 us (2%)
    psum x1, waiting for transfers between devices, shards(): lax.psum(adapter_scale * contract_leading(reduced_rank, cotangent), ('dp'...  143 us
    all_gather x1, waiting for transfers between devices, shards(): lax.all_gather(weight_reduced_float, 'fsdp', axis=0, tiled=True)  110 us
    all_to_all x1, waiting for transfers between devices, shards(): lax.all_to_all(tokens, 'fsdp', split_axis=1, concat_axis=0, tiled=True)  76.8 us
    psum x1, waiting for transfers between devices, shards(): down_factor_gradient = lax.psum(down_piece_gradient, 'dp')  68 us
    all_gather x1, waiting for transfers between devices, shards(): lax.all_gather(down_reduced_float, 'fsdp', axis=0, tiled=True)  67.3 us
    all_gather x1, waiting for transfers between devices, shards(): lax.all_gather(up_reduced_float, 'fsdp', axis=0, tiled=True)  50.9 us
    all_gather x1, waiting for transfers between devices, shards(): prior_whole = lax.all_gather(previous_up_factor, 'fsdp', axis=0, tiled=True)  36.3 us
    dot_general x3, matrix products, contract_trailing(): lax.dot_general(left, right, (((1,), (1,)), ((), ())), preferred_element_...  34.5 us
  transfers between devices with their start and end apart: 8, of which 8 were waited for; matrix products, arithmetic and copies ran while one was open for 8% of the time, Pallas kernels for 0%

commit v1 on v0

v1 whole, which is shorter than its diff:
```python
import functools

import jax
import jax.numpy as jnp
import numpy as np
from jax import lax
from jax.experimental import pallas as pl
from jax.experimental.pallas import tpu as pltpu
from jax.sharding import Mesh
from jax.sharding import PartitionSpec as P

scale = 0.25
AXES = ("y", "zl", "zh", "x", "c")
SIZES = (4, 2, 2, 4, 2)
bf16 = jnp.bfloat16
f32 = jnp.float32
VMEM = 32 * 2**20
MOST = 60 * 2**20
COST = pl.CostEstimate(flops=0, bytes_accessed=2**16, transcendentals=0)


def pairs(move):
    out = []
    for i in range(128):
        y, zl, zh, x, c = (int(v) for v in np.unravel_index(i, SIZES))
        x2, y2, z2, c2 = move(x, y, 2 * zh + zl, c)
        z2 %= 4
        j = np.ravel_multi_index((y2 % 4, z2 % 2, z2 // 2, x2 % 4, c2), SIZES)
        out.append((i, int(j)))
    return out


def sg(c):
    return 1 - 2 * c


MOVES = {
    "core": pairs(lambda x, y, z, c: (x, y, z, 1 - c)),
    "xp": pairs(lambda x, y, z, c: (x + sg(c), y, z, c)),
    "xq": pairs(lambda x, y, z, c: (x - sg(c), y, z, c)),
    "z1": pairs(lambda x, y, z, c: (x, y, 3 - z, c)),
}


def send(v, move):
    return lax.ppermute(v, AXES, MOVES[move])


def nt(a, b):
    return lax.dot_general(a, b, (((1,), (1,)), ((), ())), preferred_element_type=f32)


def tn(a, b):
    return lax.dot_general(a, b, (((0,), (0,)), ((), ())), preferred_element_type=f32)


def nn(a, b):
    return lax.dot_general(a, b, (((1,), (0,)), ((), ())), preferred_element_type=f32)


def call(kernel, name, args, out_shape, scratch, aliases={}):
    hbm = pl.BlockSpec(memory_space=pltpu.HBM)
    return pl.pallas_call(
        kernel,
        in_specs=[pl.BlockSpec(memory_space=pltpu.SMEM)] + [hbm] * (len(args) - 1),
        out_specs=[hbm] * len(out_shape),
        out_shape=[jax.ShapeDtypeStruct(*s) for s in out_shape],
        scratch_shapes=scratch,
        input_output_aliases=aliases,
        compiler_params=pltpu.CompilerParams(vmem_limit_bytes=MOST),
        cost_estimate=COST,
        name=name,
    )(*args)


def column(i):
    return pl.ds(pl.multiple_of(i * 512, 512), 512)


def start(copies):
    for cp in copies:
        cp.start()
    return copies


def wait(copies):
    for cp in copies:
        cp.wait()


def row_copies(own_hbm, sib_hbm, out, sems, c):
    n = own_hbm.shape[1]
    copies = []
    for j in range(8):
        own, sib = (pl.ds(pl.multiple_of((2 * j + i) * n, n), n) for i in (c, 1 - c))
        copies.append(pltpu.make_async_copy(own_hbm.at[j], out.at[own], sems.at[0, j]))
        copies.append(pltpu.make_async_copy(sib_hbm.at[j], out.at[sib], sems.at[1, j]))
    return copies


def cot_copies(cot_hbm, tr_hbm, out, sems):
    n = cot_hbm.shape[0]
    return [
        pltpu.make_async_copy(cot_hbm, out.at[pl.ds(0, n)], sems.at[0]),
        pltpu.make_async_copy(tr_hbm.at[:, pl.ds(4096, 1024)], out.at[pl.ds(n, n)], sems.at[1]),
    ]


def prepare_kernel(up_ref, down_ref, o_ref, d_ref):
    up = up_ref[...].astype(bf16)
    for k in range(8):
        o_ref[k] = up
    d_ref[...] = down_ref[...].astype(bf16)


def prepare(up, down):
    vm = pl.BlockSpec(memory_space=pltpu.VMEM)
    return pl.pallas_call(
        prepare_kernel,
        in_specs=[vm, vm],
        out_specs=[vm, vm],
        out_shape=[jax.ShapeDtypeStruct((8,) + up.shape, bf16), jax.ShapeDtypeStruct(down.shape, bf16)],
        cost_estimate=COST,
        name="prepare",
    )(up, down)


def pick_kernel(s_ref, t_hbm, cot_hbm, p_hbm, picked, psems, osems):
    c = s_ref[0]
    picks = start([pltpu.make_async_copy(cot_hbm, picked.at[:, pl.ds(4096, 1024)], psems.at[8])])
    for k in range(8):
        there = picked.at[:, pl.ds(512 * k, 512)]
        picks += start([pltpu.make_async_copy(t_hbm.at[:, column(2 * k + 1 - c)], there, psems.at[k])])
    outs = []
    for k in range(4):
        wait(picks[2 * k + 1 : 2 * k + 3])
        there = pl.ds(1024 * k, 1024)
        outs += start([pltpu.make_async_copy(picked.at[:, there], p_hbm.at[:, there], osems.at[k])])
    there = pl.ds(4096, 1024)
    wait(picks[:1])
    outs += start([pltpu.make_async_copy(picked.at[:, there], p_hbm.at[:, there], osems.at[4])])
    wait(outs)


def pick_columns(tokens, cot, place):
    n = tokens.shape[0]
    return call(
        pick_kernel,
        "pick_columns",
        (place, tokens, cot),
        [((n, 5120), bf16)],
        [pltpu.VMEM((n, 5120), bf16), pltpu.SemaphoreType.DMA((9,)), pltpu.SemaphoreType.DMA((5,))],
    )[0]


def rank_kernel(
    s_ref, t_hbm, tr_hbm, cot_hbm, up_hbm, ups_hbm, g_hbm, whole_hbm, br_hbm,
    whole, cot2, br, flip, tbuf, gbuf, usems, csems, tsems, gsems, osems,
):
    n = t_hbm.shape[0]
    c = s_ref[0]
    first = start(row_copies(up_hbm, ups_hbm, whole, usems, c) + cot_copies(cot_hbm, tr_hbm, cot2, csems))
    ins = []
    for k in range(8):
        there = pl.ds(512 * k, 512)
        ins.append(
            [
                pltpu.make_async_copy(t_hbm.at[:, column(2 * k + c)], tbuf.at[pl.ds(0, n), there], tsems.at[0, k]),
                pltpu.make_async_copy(tr_hbm.at[:, there], tbuf.at[pl.ds(n, n), there], tsems.at[1, k]),
            ]
        )
    wait(first)
    for k in range(3):
        start(ins[k])
    flip[...] = nt(whole[...], cot2[...]).astype(bf16)
    br[...] = nt(cot2[...], whole[...]).astype(bf16)
    outs = start(
        [
            pltpu.make_async_copy(whole, whole_hbm, osems.at[0]),
            pltpu.make_async_copy(br, br_hbm, osems.at[1]),
        ]
    )
    for k in range(8):
        wait(ins[k])
        if k + 3 < 8:
            start(ins[k + 3])
        gbuf[k] = (scale * nn(flip[...], tbuf[:, 512 * k : 512 * k + 512])).astype(bf16)
        outs += start(
            [
                pltpu.make_async_copy(gbuf.at[k, :, pl.ds(128 * j, 128)], g_hbm.at[j, k], gsems.at[j, k])
                for j in range(4)
            ]
        )
    wait(outs)


def rank_partials(tokens, tokens_sib, cot, up, up_sib, place):
    n = tokens.shape[0]
    return call(
        rank_kernel,
        "rank_partials",
        (place, tokens, tokens_sib, cot, up, up_sib),
        [((4, 8, 512, 128), bf16), ((512, 1024), bf16), ((2 * n, 512), bf16)],
        [
            pltpu.VMEM((512, 1024), bf16),
            pltpu.VMEM((2 * n, 1024), bf16),
            pltpu.VMEM((2 * n, 512), bf16),
            pltpu.VMEM((512, 2 * n), bf16),
            pltpu.VMEM((2 * n, 4096), bf16),
            pltpu.VMEM((8, 512, 512), bf16),
            pltpu.SemaphoreType.DMA((2, 8)),
            pltpu.SemaphoreType.DMA((2,)),
            pltpu.SemaphoreType.DMA((2, 8)),
            pltpu.SemaphoreType.DMA((4, 8)),
            pltpu.SemaphoreType.DMA((2,)),
        ],
    )


def low_kernel(s_ref, t_hbm, d_hbm, o_hbm, tbuf, dbuf, total, obuf, tsems, dsems, osem):
    ins = []
    for k in range(8):
        there = pl.ds(1024 * k, 1024)
        ins.append(
            start(
                [
                    pltpu.make_async_copy(d_hbm.at[there], dbuf.at[there], dsems.at[k]),
                    pltpu.make_async_copy(t_hbm.at[:, there], tbuf.at[:, there], tsems.at[k]),
                ]
            )
        )
    for k in range(8):
        wait(ins[k])
        part = nn(tbuf[:, 1024 * k : 1024 * k + 1024], dbuf[1024 * k : 1024 * k + 1024, :])
        total[...] = part if k == 0 else total[...] + part
    obuf[...] = total[...].astype(bf16)
    wait(start([pltpu.make_async_copy(obuf, o_hbm, osem.at[0])]))


def low_rank(tokens, down, place):
    n = tokens.shape[0]
    return call(
        low_kernel,
        "low_rank",
        (place, tokens, down),
        [((n, 512), bf16)],
        [
            pltpu.VMEM((n, 8192), bf16),
            pltpu.VMEM((8192, 512), bf16),
            pltpu.VMEM((n, 512), f32),
            pltpu.VMEM((n, 512), bf16),
            pltpu.SemaphoreType.DMA((8,)),
            pltpu.SemaphoreType.DMA((8,)),
            pltpu.SemaphoreType.DMA((1,)),
        ],
    )[0]


def owner_kernel(
    s_ref, g_hbm, low_hbm, lows_hbm, cot_hbm, tr_hbm, o_hbm, low2, cot2, gbuf, up, obuf, lsems, csems, gsems, osems
):
    n = low_hbm.shape[0]
    c = s_ref[0]
    first = start(
        [
            pltpu.make_async_copy(low_hbm, low2.at[pl.ds(0, n)], lsems.at[0]),
            pltpu.make_async_copy(lows_hbm, low2.at[pl.ds(n, n)], lsems.at[1]),
        ]
        + cot_copies(cot_hbm, tr_hbm, cot2, csems)
    )
    ins = [start([pltpu.make_async_copy(g_hbm.at[:, k], gbuf.at[k], gsems.at[k])]) for k in range(8)]
    wait(first)
    up[...] = (scale * tn(low2[...], cot2[...])).astype(bf16)
    outs = []
    for k in range(8):
        wait(ins[k])
        g = gbuf[k].astype(f32)
        g = ((g[0] + g[1]) + (g[2] + g[3])).astype(bf16)
        rows = up[pl.ds(pl.multiple_of(64 * k + 32 * c, 32), 32), :]
        for zl in range(2):
            obuf[2 * k + zl, :256] = g[256 * zl : 256 * zl + 256]
            for j in range(4):
                cols = 512 * zl + 128 * j
                obuf[2 * k + zl, 256 + 32 * j : 288 + 32 * j] = rows[:, cols : cols + 128]
        there = pl.ds(2 * k, 2)
        outs += start([pltpu.make_async_copy(obuf.at[there], o_hbm.at[there], osems.at[k])])
    wait(outs)


def owner_pieces(g, low, low_sib, cot, tokens_sib, place):
    n = low.shape[0]
    return call(
        owner_kernel,
        "owner_pieces",
        (place, g, low, low_sib, cot, tokens_sib),
        [((16, 384, 128), bf16)],
        [
            pltpu.VMEM((2 * n, 512), bf16),
            pltpu.VMEM((2 * n, 1024), bf16),
            pltpu.VMEM((8, 4, 512, 128), bf16),
            pltpu.VMEM((512, 1024), bf16),
            pltpu.VMEM((16, 384, 128), bf16),
            pltpu.SemaphoreType.DMA((2,)),
            pltpu.SemaphoreType.DMA((2,)),
            pltpu.SemaphoreType.DMA((8,)),
            pltpu.SemaphoreType.DMA((8,)),
        ],
    )[0]


def place_rows(out_ref, own_ref, sib_ref, c):
    n = own_ref.shape[1]
    for j in range(8):
        own, sib = (pl.multiple_of((2 * j + i) * n, n) for i in (c, 1 - c))
        out_ref[pl.ds(own, n), :] = own_ref[j].astype(out_ref.dtype)
        out_ref[pl.ds(sib, n), :] = sib_ref[j].astype(out_ref.dtype)


def merge_kernel(s_ref, m_ref, a_ref, b_ref, bs_ref, o_ref, w_ref, prior):
    place_rows(prior, b_ref, bs_ref, s_ref[0])
    for j in range(4):
        cols = slice(256 * j, 256 * j + 256)
        add = lax.dot_general(
            a_ref[...], prior[:, cols], (((1,), (0,)), ((), ())),
            precision=lax.Precision.HIGHEST, preferred_element_type=f32,
        )
        out = m_ref[:, cols] + scale * add
        o_ref[:, cols] = out
        w_ref[:, cols] = out.astype(bf16)


def merge(master, prev_down, prior, prior_sib, place):
    whole = pl.BlockSpec((512, 1024), lambda i: (0, 0))
    first = pl.BlockSpec((8, 32, 1024), lambda i: (0, 0, 0))
    return pl.pallas_call(
        merge_kernel,
        grid=(1,),
        in_specs=[
            pl.BlockSpec(memory_space=pltpu.SMEM),
            whole,
            pl.BlockSpec((512, 512), lambda i: (0, 0)),
            first,
            first,
        ],
        out_specs=[whole] * 2,
        out_shape=[jax.ShapeDtypeStruct((512, 1024), f32), jax.ShapeDtypeStruct((512, 1024), bf16)],
        scratch_shapes=[pltpu.VMEM((512, 1024), f32)],
        compiler_params=pltpu.CompilerParams(vmem_limit_bytes=VMEM),
        cost_estimate=COST,
        name="merge",
    )(place, master, prev_down, prior, prior_sib)


def main_kernel(units, before, s_ref, t_hbm, tr_hbm, d_hbm, cot_hbm, br_hbm, *rest):
    n = t_hbm.shape[0]
    w_hbm, rest = rest[:units], rest[units:]
    if before:
        (v_hbm, _, r_hbm), rest = rest[:3], rest[3:]
    vo_hbm, vs_hbm, x_hbm, o_hbm, cot2, br, tbuf, wbuf, dbuf, xbuf, vbuf, lbuf, rest = *rest[:12], rest[12:]
    csems, tsems, wsems, osems, vsems, rsems = rest

    def span(u):
        return pl.ds(512 * u, 512)

    late = []
    if before:
        late = [pltpu.make_async_copy(r_hbm, lbuf, rsems.at[before])]
    ins, tokens = [], []
    for u in range(units):
        ins.append(
            [
                pltpu.make_async_copy(w_hbm[u], wbuf.at[span(u)], wsems.at[0, u]),
                pltpu.make_async_copy(d_hbm.at[column(s_ref[u])], dbuf.at[u], wsems.at[1, u]),
            ]
        )
        here = t_hbm.at[:, column(s_ref[u])]
        there = tr_hbm.at[:, column(s_ref[units + u])]
        tokens.append(pltpu.make_async_copy(here, tbuf.at[pl.ds(0, n), span(u)], tsems.at[0, u]))
        tokens.append(pltpu.make_async_copy(there, tbuf.at[pl.ds(n, n), span(u)], tsems.at[1, u]))
    if before:
        late.append(pltpu.make_async_copy(v_hbm[0], vbuf.at[pl.ds(0, n)], vsems.at[0, 4]))
        late.append(pltpu.make_async_copy(v_hbm[1], vbuf.at[pl.ds(n, n)], vsems.at[1, 4]))
    first = start(cot_copies(cot_hbm, tr_hbm, cot2, csems) + [pltpu.make_async_copy(br_hbm, br, csems.at[2])])
    start(ins[0])
    wait(first)
    outs = []
    for u in range(units):
        wait(ins[u])
        if u + 1 < units:
            start(ins[u + 1])
        else:
            start(late)
        start(tokens[2 * u : 2 * u + 2])
        x = nt(cot2[...], wbuf[512 * u : 512 * u + 512, :]) + scale * nt(br[...], dbuf[u])
        xbuf[u] = x.astype(bf16)
        outs += start(
            [
                pltpu.make_async_copy(xbuf.at[u, pl.ds(0, n)], x_hbm.at[:, column(s_ref[u])], osems.at[0, u]),
                pltpu.make_async_copy(xbuf.at[u, pl.ds(n, n)], o_hbm.at[:, span(u)], osems.at[1, u]),
            ]
        )
    wait(late)
    for u in range(before):
        there = x_hbm.at[:, column(s_ref[2 * units + u])]
        outs += start([pltpu.make_async_copy(lbuf.at[:, span(u)], there, rsems.at[u])])
    wait(tokens)
    for j in range(4):
        cols = slice(256 * j, 256 * j + 256)
        there = pl.ds(256 * j, 256)
        part = nn(tbuf[...], wbuf[:, cols])
        vbuf[:, cols] = part + vbuf[:, cols] if before else part
        outs += start(
            [
                pltpu.make_async_copy(vbuf.at[pl.ds(0, n), there], vo_hbm.at[:, there], vsems.at[0, j]),
                pltpu.make_async_copy(vbuf.at[pl.ds(n, n), there], vs_hbm.at[:, there], vsems.at[1, j]),
            ]
        )
    wait(outs)


def main_group(tokens, tokens_sib, down, cot, br2, blocks, starts, before=0, carry=()):
    n, d = tokens.shape
    units = len(blocks)
    args = [starts, tokens, tokens_sib, down, cot, br2, *blocks]
    kernel = main_kernel
    aliases = {}
    if before:
        aliases = {len(args) + 2: 2}
        args += list(carry)

        def kernel(units, before, *refs):
            at = 6 + units
            refs = refs[:at] + ((refs[at], refs[at + 1]),) + refs[at + 2 :]
            main_kernel(units, before, *refs)

    return call(
        functools.partial(kernel, units, before),
        "main_group",
        args,
        [((n, 1024), f32), ((n, 1024), f32), ((n, d), bf16), ((n, 512 * units), bf16)],
        [
            pltpu.VMEM((2 * n, 1024), bf16),
            pltpu.VMEM((2 * n, 512), bf16),
            pltpu.VMEM((2 * n, 512 * units), bf16),
            pltpu.VMEM((512 * units, 1024), bf16),
            pltpu.VMEM((units, 512, 512), bf16),
            pltpu.VMEM((units, 2 * n, 512), bf16),
            pltpu.VMEM((2 * n, 1024), f32),
            pltpu.VMEM((n, 512 * max(before, 1)), bf16),
            pltpu.SemaphoreType.DMA((3,)),
            pltpu.SemaphoreType.DMA((2, units)),
            pltpu.SemaphoreType.DMA((2, units)),
            pltpu.SemaphoreType.DMA((2, units)),
            pltpu.SemaphoreType.DMA((2, 5)),
            pltpu.SemaphoreType.DMA((before + 1,)),
        ],
        aliases,
    )


def sum_kernel(in_ref, o_ref):
    total = in_ref[0].astype(f32)
    for k in range(1, 16):
        total = total + in_ref[k].astype(f32)
    down = total[:256].T
    up = total[256:]
    for k in range(8):
        o_ref[k, :128] = down
        for j in range(2):
            o_ref[k, 128 + 32 * j : 160 + 32 * j, :128] = up[64 * j : 64 * j + 32]
            o_ref[k, 128 + 32 * j : 160 + 32 * j, 128:] = up[64 * j + 32 : 64 * j + 64]


def sum_pieces(pieces):
    vm = pl.BlockSpec(memory_space=pltpu.VMEM)
    return pl.pallas_call(
        sum_kernel,
        in_specs=[vm],
        out_specs=vm,
        out_shape=jax.ShapeDtypeStruct((8, 192, 256), f32),
        compiler_params=pltpu.CompilerParams(vmem_limit_bytes=VMEM),
        cost_estimate=COST,
        name="sum_pieces",
    )(pieces)


def join_kernel(in_ref, down_ref, up_ref):
    for y in range(4):
        for zl in range(2):
            down_ref[128 * y : 128 * y + 128, 256 * zl : 256 * zl + 256] = in_ref[2 * y + zl, :128]
    for zl in range(2):
        for j in range(2):
            rows = slice(128 + 32 * j, 160 + 32 * j)
            total = in_ref[zl, rows] + in_ref[2 + zl, rows] + in_ref[4 + zl, rows] + in_ref[6 + zl, rows]
            up_ref[:, 512 * zl + 256 * j : 512 * zl + 256 * j + 256] = total


def join_pieces(pieces):
    vm = pl.BlockSpec(memory_space=pltpu.VMEM)
    return pl.pallas_call(
        join_kernel,
        in_specs=[vm],
        out_specs=[vm, vm],
        out_shape=[jax.ShapeDtypeStruct((512, 512), f32), jax.ShapeDtypeStruct((32, 1024), f32)],
        compiler_params=pltpu.CompilerParams(vmem_limit_bytes=VMEM),
        cost_estimate=COST,
        name="join_pieces",
    )(pieces)


def finish_kernel(
    s_ref, t_hbm, d_hbm, w_hbm, ws_hbm, cot_hbm, br_hbm, vo_hbm, vr_hbm, low_hbm, up_hbm, r_hbm, x_in,
    v_hbm, x_hbm, tbuf, wbuf, dbuf, xbuf, cot, br, vo, vr, low, up, vbuf, lbuf, sems, wsems, xsems, vsems,
):
    n = cot.shape[0]
    late = [pltpu.make_async_copy(r_hbm, lbuf, sems.at[0])]
    first = start(
        [
            pltpu.make_async_copy(cot_hbm, cot, sems.at[1]),
            pltpu.make_async_copy(br_hbm.at[pl.ds(0, n)], br, sems.at[2]),
        ]
    )
    ins, tokens = [], []
    for i, w in enumerate((w_hbm, ws_hbm)):
        there = pl.ds(512 * i, 512)
        ins.append(
            [
                pltpu.make_async_copy(w, wbuf.at[there], wsems.at[0, i]),
                pltpu.make_async_copy(d_hbm.at[column(s_ref[i])], dbuf.at[i], wsems.at[1, i]),
            ]
        )
        tokens.append(pltpu.make_async_copy(t_hbm.at[:, column(s_ref[i])], tbuf.at[:, there], wsems.at[2, i]))
    rest = tokens + [
        pltpu.make_async_copy(low_hbm, low, sems.at[3]),
        pltpu.make_async_copy(up_hbm, up, sems.at[4]),
        pltpu.make_async_copy(vo_hbm, vo, sems.at[5]),
        pltpu.make_async_copy(vr_hbm, vr, sems.at[6]),
    ]
    start(ins[0])
    wait(first)
    outs = []
    for i in range(2):
        wait(ins[i])
        start(late + ins[1] if i == 0 else rest)
        x = nt(cot[...], wbuf[512 * i : 512 * i + 512, :]) + scale * nt(br[...], dbuf[i])
        xbuf[i] = x.astype(bf16)
        outs += start([pltpu.make_async_copy(xbuf.at[i], x_hbm.at[:, column(s_ref[i])], xsems.at[i])])
    wait(late)
    for u in range(3):
        there = x_hbm.at[:, column(s_ref[2 + u])]
        outs += start([pltpu.make_async_copy(lbuf.at[:, pl.ds(512 * u, 512)], there, xsems.at[2 + u])])
    wait(rest)
    for j in range(4):
        cols = slice(256 * j, 256 * j + 256)
        there = pl.ds(256 * j, 256)
        v = nn(tbuf[...], wbuf[:, cols]) + scale * nn(low[...], up[:, cols])
        vbuf[:, cols] = (vo[:, cols] + vr[:, cols] + v).astype(bf16)
        outs += start([pltpu.make_async_copy(vbuf.at[:, there], v_hbm.at[:, there], vsems.at[j])])
    wait(outs)


def finish(x, recv, tokens, down, w, w_sib, cot, br2, vo, vr, low, up, starts):
    n, d = x.shape
    return call(
        finish_kernel,
        "finish",
        (starts, tokens, down, w, w_sib, cot, br2, vo, vr, low, up, recv, x),
        [((n, 1024), bf16), ((n, d), bf16)],
        [
            pltpu.VMEM((n, 1024), bf16),
            pltpu.VMEM((1024, 1024), bf16),
            pltpu.VMEM((2, 512, 512), bf16),
            pltpu.VMEM((2, n, 512), bf16),
            pltpu.VMEM((n, 1024), bf16),
            pltpu.VMEM((n, 512), bf16),
            pltpu.VMEM((n, 1024), f32),
            pltpu.VMEM((n, 1024), f32),
            pltpu.VMEM((n, 512), bf16),
            pltpu.VMEM((512, 1024), bf16),
            pltpu.VMEM((n, 1024), bf16),
            pltpu.VMEM((n, 1536), bf16),
            pltpu.SemaphoreType.DMA((7,)),
            pltpu.SemaphoreType.DMA((3, 2)),
            pltpu.SemaphoreType.DMA((5,)),
            pltpu.SemaphoreType.DMA((4,)),
        ],
        {12: 1},
    )


def shards(tokens, master, prev_down, prev_up, fresh_down, fresh_up, cot):
    y, zl, zh, x, c = (lax.axis_index(a) for a in AXES)
    bar = lax.optimization_barrier
    place = jnp.stack([c, zh, x])

    def to_owners(v, axes):
        return lax.all_to_all(v, axes, split_axis=0, concat_axis=0)

    def first_step(v):
        return send(v, "xp"), send(v, "xq"), send(v, "z1")

    def second_step(p, q, far):
        return send(p, "xp"), send(far, "xq"), send(p, "z1")

    def first_step(v):
        return send(v, "xp"), send(v, "xq"), send(v, "z1")

    def second_step(p, q, far):
        return send(p, "xp"), send(far, "xq"), send(p, "z1")

    copies, down_half = prepare(fresh_up, fresh_down)
    copies, down_half, place = bar((copies, down_half, place))
    up = to_owners(copies, ("zh", "x"))
    down = lax.all_gather(down_half, ("zh", "x", "c"), axis=0, tiled=True)
    tokens_sib = send(pick_columns(tokens, cot, place), "core")
    prior = jnp.broadcast_to(prev_up[None], (8,) + prev_up.shape)
    up, prior, tokens_sib = bar((up, prior, tokens_sib))
    up_sib = send(up, "core")

    prior = to_owners(prior, ("zh", "x"))
    g, up_rows, br2 = rank_partials(tokens, tokens_sib, cot, up, up_sib, place)
    prior, g = bar((prior, g))
    prior_sib = send(prior, "core")
    g = to_owners(g, ("y",))

    merged, w = merge(master, prev_down, prior, prior_sib, place)
    p, q, far = bar(first_step(w))
    second = second_step(p, q, far)

    def blocks_of(core):
        s = 1 - 2 * core
        p, q, r = (x - s) % 4, (x + s) % 4, (x + 2) % 4
        here, there = 4 * zh, 4 * (1 - zh)
        one = jnp.stack([here + x, here + p, here + q, there + x])
        two = jnp.stack([here + r, there + p, there + q])
        return one, two, (there + r)[None]

    own = blocks_of(c)
    sib = [2 * k + 1 - c for k in blocks_of(1 - c)]
    starts = [
        jnp.concatenate([2 * own[0] + c, own[0]]),
        jnp.concatenate([2 * own[1] + c, own[1], sib[0]]),
        jnp.concatenate([2 * own[2] + c, sib[2], sib[1]]),
    ]
    starts = [v.astype(jnp.int32) for v in starts]

    low = low_rank(tokens, down, place)
    pieces = owner_pieces(g, low, send(low, "core"), cot, tokens_sib, place)
    shared = (tokens, tokens_sib, down, cot, br2)
    pieces, p = bar((pieces, p))
    part = main_group(*shared, [w, p, q, far], starts[0])
    r, far_q, far_p, part = bar(second + (part,))

    far_r = send(far_q, "xq")
    pieces = to_owners(pieces, ("zh", "x", "zl"))
    vo, vs, dx, other = part
    part = main_group(*shared, [r, far_p, far_q], starts[1], 4, (vo, vs, dx, send(other, "core")))
    part, pieces = bar((part, sum_pieces(pieces)))

    pieces = to_owners(pieces, ("y", "zl"))
    vo, vs, dx, other = part
    values, dx = finish(
        dx, send(other, "core"), tokens, down, far_r, send(far_r, "core"), cot, br2, vo, send(vs, "core"), low, up_rows, starts[2]
    )
    down_grad, up_grad = join_pieces(pieces)
    return merged, values, dx, down_grad, up_grad


def solution(mesh):
    fine = Mesh(mesh.devices.reshape(SIZES), AXES)
    dp, fsdp = ("y", "zl"), ("zh", "x", "c")
    rows, owned = P(dp + fsdp, None), P(fsdp, None)
    return jax.shard_map(
        shards,
        mesh=fine,
        in_specs=(rows, owned, owned, owned, owned, owned, rows),
        out_specs=(owned, rows, rows, owned, owned),
        check_vma=False,
    )
```

time: 668 us -> 207 us (0.31)
  waiting for transfers between devices: 561 us -> 48.1 us
  matrix products: 73.7 us -> 0 us
  Pallas kernels: 0 us -> 71.1 us
  starting transfers between devices: 5.05 us -> 40.6 us
  blocking collectives: 0 us -> 20.2 us
    all_gather x5 -> x1, waiting for transfers between devices: 272 us -> 0.01 us  [shards(): down = lax.all_gather(down_half, ('zh', 'x', 'c'), axis=0, tiled=True)]
    psum x2 -> x0, waiting for transfers between devices: 211 us -> none  [the longest x1 143 us: shards(): lax.psum(adapter_scale * contract_leading(reduced_rank, cotangent), ('dp'...]
    dot_general x9 -> x0, matrix products: 73.7 us -> none  [the longest x3 34.5 us: contract_trailing(): lax.dot_general(left, right, (((1,), (1,)), ((), ())), preferred_element_...]
    pallas_call x0 -> x11, Pallas kernels: none -> 71.1 us  [the longest x7 60.7 us: call(): pl.pallas_call(kernel, in_specs=[pl.BlockSpec(memory_space=pltpu.SMEM)] +...]
    all_to_all x1 -> x4, waiting for transfers between devices: 76.8 us -> 8.96 us  [to_owners(): return lax.all_to_all(v, axes, split_axis=0, concat_axis=0)]
    ppermute x0 -> x15, waiting for transfers between devices: none -> 39.1 us  [send(): return lax.ppermute(v, AXES, MOVES[move])]
    ppermute x0 -> x15, starting transfers between devices: none -> 22.7 us  [send(): return lax.ppermute(v, AXES, MOVES[move])]
    all_to_all x0 -> x1, blocking collectives: none -> 20.2 us  [to_owners(): return lax.all_to_all(v, axes, split_axis=0, concat_axis=0)]
  transfers between devices with their start and end apart: 8 -> 20, of which waited for: 8 -> 10; matrix products, arithmetic and copies ran while one was open for 8% -> 2% of each run, Pallas kernels for 0% -> 33%
where the time goes in v1:
time: 207 us; the launch traced here: 205 us
  Pallas kernels  71.1 us (34%)
  waiting for transfers between devices  48.1 us (23%)
  starting transfers between devices  40.6 us (20%)
  blocking collectives  20.2 us (10%)
  between operations  14.3 us (7%)
  local copies, waits for them, and re-layouts  9.16 us (4%)
    pallas_call x7, Pallas kernels, call(): pl.pallas_call(kernel, in_specs=[pl.BlockSpec(memory_space=pltpu.SMEM)] +...  60.7 us
    ppermute x15, waiting for transfers between devices, send(): return lax.ppermute(v, AXES, MOVES[move])  39.1 us
    ppermute x15, starting transfers between devices, send(): return lax.ppermute(v, AXES, MOVES[move])  22.7 us
    all_to_all x1, blocking collectives, to_owners(): return lax.all_to_all(v, axes, split_axis=0, concat_axis=0)  20.2 us
    all_to_all x4, starting transfers between devices, to_owners(): return lax.all_to_all(v, axes, split_axis=0, concat_axis=0)  17.8 us
    all_to_all x4, waiting for transfers between devices, to_owners(): return lax.all_to_all(v, axes, split_axis=0, concat_axis=0)  8.96 us
    unnamed x26, local copies, waits for them, and re-layouts  6.83 us
    pallas_call x1, Pallas kernels, merge(): pl.pallas_call(merge_kernel, grid=(1,), in_specs=[pl.BlockSpec(memory_spa...  5.51 us
  transfers between devices with their start and end apart: 20, of which 10 were waited for; matrix products, arithmetic and copies ran while one was open for 2% of the time, Pallas kernels for 33%

profile of v1, /device:TPU:1, one launch (start us, length us, event | category | flops | bytes accessed | tf_op | source)
XLA Modules:
  0.0 204.8 jit_solution(13986786405919642652)
XLA Ops:
  7.2 2.3 %prepare.1 = (bf16[8,32,1024]{2,1,0:T(8,128)(2,1)}, bf16[512,512]{1,0:T(8,128)(2,1)}) custom-call(f32[32,1024]{1,0:T(8,128)} %up_ref.1, f32[512,512]{1,0:T(8,128)} %down_ref.1), custom_call_target="tpu_custom_call" | custom-call | bytes 65536 | tf_op jit(solution)/shard_map/prepare/pallas_call | solution.py:118
  10.2 3.9 %pick_columns.1 = bf16[320,5120]{1,0:T(8,128)(2,1)} custom-call(s32[3]{0:T(128)} %pad_add_fusion.s_ref, bf16[320,8192]{1,0:T(8,128)(2,1)} %t_hbm.9, bf16[320,1024]{1,0:T(8,128)(2,1)} %cot_hbm.9), custom_call_target="tpu_custom_call" | custom-call | bytes 65536 | tf_op jit(solution)/shard_map/pick_columns/pallas_call | solution.py:63
  15.6 20.2 %all_to_all.25.up_hbm = bf16[8,32,1024]{2,1,0:T(8,128)(2,1)S(1)} all-to-all(bf16[8,32,1024]{2,1,0:T(8,128)(2,1)S(1)} %copy-done.10), channel_id=1, replica_groups=mesh['y'=4,'zl'=2,'zh'=2,'x'=4,'c'=2] {'zh','x'}, dimensions={0} | all-to-all | bytes 1048576 | tf_op jit(solution)/shard_map/all_to_all | solution.py:597
  36.9 4.4 %all-to-all-start.1 = ((f32[8,32,1024]{2,1,0:T(8,128)}), f32[8,32,1024]{2,1,0:T(8,128)S(1)}, u32[]{:S(2)}, u32[]{:S(2)}) async-start(f32[8,32,1024]{2,1,0:T(8,128)} %broadcast_in_dim.2), calls=%async_computation.1 | async-start | bytes 2097152 | tf_op jit(solution)/shard_map/all_to_all | solution.py:597
  41.3 2.6 %collective-permute-start.1 = (bf16[8,32,1024]{2,1,0:T(8,128)(2,1)S(1)}, bf16[8,32,1024]{2,1,0:T(8,128)(2,1)S(1)}, u32[]{:S(2)}, u32[]{:S(2)}) collective-permute-start(bf16[8,32,1024]{2,1,0:T(8,128)(2,1)S(1)} %all_to_all.25.up_hbm), channel_id=1, source_target_pairs={{0,1},{1,0},{2,3},{3,2},{4,5},{5,4},{6,7},{7,6},{8,9},{9,8},{10,11... | collective-permute-start | bytes 1572872 | tf_op jit(solution)/shard_map/ppermute | solution.py:46
  46.2 10.9 %rank_partials.1 = (bf16[4,8,512,128]{3,2,1,0:T(8,128)(2,1)}, bf16[512,1024]{1,0:T(8,128)(2,1)}, bf16[640,512]{1,0:T(8,128)(2,1)}) custom-call(s32[3]{0:T(128)} %pad_add_fusion.s_ref, bf16[320,8192]{1,0:T(8,128)(2,1)} %t_hbm.9, bf16[320,5120]{1,0:T(8,128)(2,1)} %collective-permute-done.tr_hbm.refs_2_, bf16[320,1024]{1,0:T(8,128)(2,1)} %cot_hbm.9, ...), custom_call_target="tpu_custom_call" | custom-call | bytes 65536 | tf_op jit(solution)/shard_map/rank_partials/pallas_call | solution.py:63
  57.1 2.1 %all-to-all-done.1.b_ref = f32[8,32,1024]{2,1,0:T(8,128)S(1)} async-done(((f32[8,32,1024]{2,1,0:T(8,128)}), f32[8,32,1024]{2,1,0:T(8,128)S(1)}, u32[]{:S(2)}, u32[]{:S(2)}) %all-to-all-start.1) | async-done | bytes 1048608 | tf_op jit(solution)/shard_map/all_to_all | solution.py:597
  59.2 5.0 %all-to-all-start.2 = ((bf16[4,8,512,128]{3,2,1,0:T(8,128)(2,1)}), bf16[4,8,512,128]{3,2,1,0:T(8,128)(2,1)}, u32[]{:S(2)}, u32[]{:S(2)}) async-start(bf16[4,8,512,128]{3,2,1,0:T(8,128)(2,1)} %get-tuple-element.64), calls=%async_computation.2 | async-start | bytes 8388608 | tf_op jit(solution)/shard_map/all_to_all | solution.py:597
  64.2 2.0 collective-permute-start.2
  66.2 2.3 %collective-permute-done.2.bs_ref = f32[8,32,1024]{2,1,0:T(8,128)S(1)} collective-permute-done((f32[8,32,1024]{2,1,0:T(8,128)S(1)}, f32[8,32,1024]{2,1,0:T(8,128)S(1)}, u32[]{:S(2)}, u32[]{:S(2)}) %collective-permute-start.2) | collective-permute-done | bytes 1048608 | tf_op jit(solution)/shard_map/ppermute | solution.py:46
  69.7 5.5 %merge.1 = (f32[512,1024]{1,0:T(8,128)}, bf16[512,1024]{1,0:T(8,128)(2,1)S(1)}) custom-call(s32[3]{0:T(128)S(1)} %copy-done.3, f32[512,1024]{1,0:T(8,128)S(1)} %copy-done, f32[512,512]{1,0:T(8,128)S(1)} %copy-done.2, f32[8,32,1024]{2,1,0:T(8,128)S(1)} %all-to-all-done.1.b_ref, f32[8,32,1024]{2,1,0:T(8,128)S(1)} %collective-permute-done.2.bs_ref), custom_call_target="tpu_custom_call" | custom-call | bytes 65536 | tf_op jit(solution)/shard_map/merge/pallas_call | solution.py:335
  77.1 3.0 %collective-permute-start.5 = (bf16[512,1024]{1,0:T(8,128)(2,1)S(1)}, bf16[512,1024]{1,0:T(8,128)(2,1)}, u32[]{:S(2)}, u32[]{:S(2)}) collective-permute-start(bf16[512,1024]{1,0:T(8,128)(2,1)S(1)} %get-tuple-element.60.rest_0_), channel_id=1, source_target_pairs={{0,24},{1,25},{2,26},{3,27},{4,28},{5,29},{6,30},{7,31},{8,16},{9,... | collective-permute-start | bytes 3145736 | tf_op jit(solution)/shard_map/ppermute | solution.py:46
  80.2 26.8 %collective-permute-done.3.rest_1_ = bf16[512,1024]{1,0:T(8,128)(2,1)} collective-permute-done((bf16[512,1024]{1,0:T(8,128)(2,1)S(1)}, bf16[512,1024]{1,0:T(8,128)(2,1)}, u32[]{:S(2)}, u32[]{:S(2)}) %collective-permute-start.3) | collective-permute-done | bytes 1048608 | tf_op jit(solution)/shard_map/ppermute | solution.py:46
  111.4 2.6 %collective-permute-start.8 = (bf16[512,1024]{1,0:T(8,128)(2,1)}, bf16[512,1024]{1,0:T(8,128)(2,1)}, u32[]{:S(2)}, u32[]{:S(2)}) collective-permute-start(bf16[512,1024]{1,0:T(8,128)(2,1)} %collective-permute-done.3.rest_1_), channel_id=1, source_target_pairs={{0,24},{1,25},{2,26},{3,27},{4,28},{5,29},{6,30},{7,31},{8,16},{9,... | collective-permute-start | bytes 3145736 | tf_op jit(solution)/shard_map/ppermute | solution.py:46
  114.0 6.9 %low_rank.1.low_hbm = bf16[320,512]{1,0:T(8,128)(2,1)} custom-call(s32[3]{0:T(128)} %pad_add_fusion.s_ref, bf16[320,8192]{1,0:T(8,128)(2,1)} %t_hbm.9, bf16[8192,512]{1,0:T(8,128)(2,1)} %all-gather.2.cloned.1.call-done.d_hbm.refs_3_), custom_call_target="tpu_custom_call" | custom-call | bytes 65536 | tf_op jit(solution)/shard_map/low_rank/pallas_call | solution.py:63
  124.7 5.7 %owner_pieces.1 = bf16[16,384,128]{2,1,0:T(8,128)(2,1)} custom-call(s32[3]{0:T(128)} %pad_add_fusion.s_ref, bf16[4,8,512,128]{3,2,1,0:T(8,128)(2,1)} %all-to-all-done.2.g_hbm, bf16[320,512]{1,0:T(8,128)(2,1)} %low_rank.1.low_hbm, bf16[320,512]{1,0:T(8,128)(2,1)} %copy-done.11, bf16[320,1024]{1,0:T(8,128)(2,1)} %cot_hbm.9, ...), custom_call_target="tpu_custom_call" | custom-call | bytes 65536 | tf_op jit(solution)/shard_map/owner_pieces/pallas_call | solution.py:63
  130.4 3.7 %all-to-all-start.3 = ((bf16[16,384,128]{2,1,0:T(8,128)(2,1)}), bf16[16,384,128]{2,1,0:T(8,128)(2,1)S(1)}, u32[]{:S(2)}, u32[]{:S(2)}) async-start(bf16[16,384,128]{2,1,0:T(8,128)(2,1)} %owner_pieces.1), calls=%async_computation.3 | async-start | bytes 3145728 | tf_op jit(solution)/shard_map/all_to_all | solution.py:597
  134.9 12.6 %main_group.2 = (f32[320,1024]{1,0:T(8,128)}, f32[320,1024]{1,0:T(8,128)}, bf16[320,8192]{1,0:T(8,128)(2,1)}, bf16[320,2048]{1,0:T(8,128)(2,1)}) custom-call(s32[8]{0:T(128)} %concatenate.12.s_ref, bf16[320,8192]{1,0:T(8,128)(2,1)} %t_hbm.9, bf16[320,5120]{1,0:T(8,128)(2,1)} %collective-permute-done.tr_hbm.refs_2_, ...), custom_call_target="tpu_custom_call" | custom-call | bytes 65536 | tf_op jit(solution)/shard_map/main_group/pallas_call | solution.py:63
  148.5 3.1 %collective-permute-start.12 = (bf16[320,2048]{1,0:T(8,128)(2,1)}, bf16[320,2048]{1,0:T(8,128)(2,1)S(1)}, u32[]{:S(2)}, u32[]{:S(2)}) collective-permute-start(bf16[320,2048]{1,0:T(8,128)(2,1)} %get-tuple-element.77), channel_id=1, source_target_pairs={{0,1},{1,0},{2,3},{3,2},{4,5},{5,4},{6,7},{7,6},{8,9},{9,8},{10,11... | collective-permute-start | bytes 3932168 | tf_op jit(solution)/shard_map/ppermute | solution.py:46
  155.5 11.8 %main_group.3 = (f32[320,1024]{1,0:T(8,128)}, f32[320,1024]{1,0:T(8,128)}, bf16[320,8192]{1,0:T(8,128)(2,1)}, bf16[320,1536]{1,0:T(8,128)(2,1)}) custom-call(s32[10]{0:T(128)} %concatenate.13.refs_0_, bf16[320,8192]{1,0:T(8,128)(2,1)} %t_hbm.9, bf16[320,5120]{1,0:T(8,128)(2,1)} %collective-permute-done.tr_hbm.refs_2_, ...), custom_call_target="tpu_custom_call", output_to_operand_aliasing={{2}: (11, {})} | custom-call | bytes 65536 | tf_op jit(solution)/shard_map/main_group/pallas_call | solution.py:63
  168.8 4.7 %all-to-all-start.4 = ((f32[8,192,256]{2,1,0:T(8,128)}), f32[8,192,256]{2,1,0:T(8,128)S(1)}, u32[]{:S(2)}, u32[]{:S(2)}) async-start(f32[8,192,256]{2,1,0:T(8,128)} %sum_pieces.1), calls=%async_computation.4 | async-start | bytes 3145728 | tf_op jit(solution)/shard_map/all_to_all | solution.py:597
  175.3 3.3 %collective-permute-done.11.ws_hbm = bf16[512,1024]{1,0:T(8,128)(2,1)} collective-permute-done((bf16[512,1024]{1,0:T(8,128)(2,1)}, bf16[512,1024]{1,0:T(8,128)(2,1)}, u32[]{:S(2)}, u32[]{:S(2)}) %collective-permute-start.11) | collective-permute-done | bytes 1048608 | tf_op jit(solution)/shard_map/ppermute | solution.py:46
  181.1 8.8 %finish.1 = (bf16[320,1024]{1,0:T(8,128)(2,1)}, bf16[320,8192]{1,0:T(8,128)(2,1)}) custom-call(s32[5]{0:T(128)} %pad_add_fusion.1.s_ref, bf16[320,8192]{1,0:T(8,128)(2,1)} %t_hbm.9, bf16[8192,512]{1,0:T(8,128)(2,1)} %all-gather.2.cloned.1.call-done.d_hbm.refs_3_, bf16[512,1024]{1,0:T(8,128)(2,1)} %collective-permute-done.10.w_hbm, ...), custom_call_target="tpu_custom_call", output_to_operand_aliasing={{1}: (12, {})} | custom-call | bytes 65536 | tf_op jit(solution)/shard_map/finish/pallas_call | solution.py:63
  190.0 6.9 %all-to-all-done.4.in_ref = f32[8,192,256]{2,1,0:T(8,128)S(1)} async-done(((f32[8,192,256]{2,1,0:T(8,128)}), f32[8,192,256]{2,1,0:T(8,128)S(1)}, u32[]{:S(2)}, u32[]{:S(2)}) %all-to-all-start.4) | async-done | bytes 1572896 | tf_op jit(solution)/shard_map/all_to_all | solution.py:597
  (64 shorter events, 29.4 us)
Async XLA Ops:
  7.2 106.8 %all-gather.2.cloned.1.call-start = ((), (), s32[]{:S(2)}) async-start(), calls=%async_computation.5 | async-start | bytes 8912896 | tf_op jit(solution)/shard_map/all_gather | solution.py:614
  10.1 25.6 %copy-start.12 = (f32[32,1024]{1,0:T(8,128)S(1)}, f32[32,1024]{1,0:T(8,128)}, u32[]{:S(2)}) copy-start(f32[32,1024]{1,0:T(8,128)} %param.10) | copy-start | bytes 393220
  14.1 21.7 %collective-permute-start = (bf16[320,5120]{1,0:T(8,128)(2,1)}, bf16[320,5120]{1,0:T(8,128)(2,1)}, u32[]{:S(2)}, u32[]{:S(2)}) collective-permute-start(bf16[320,5120]{1,0:T(8,128)(2,1)} %pick_columns.1), channel_id=1, source_target_pairs={{0,1},{1,0},{2,3},{3,2},{4,5},{5,4},{6,7},{7,6},{8,9},{9,8},{10,11... | collective-permute-start | bytes 9830408 | tf_op jit(solution)/shard_map/ppermute | solution.py:46
  35.7 9.7 %copy-start.4 = (bf16[8,32,1024]{2,1,0:T(8,128)(2,1)}, bf16[8,32,1024]{2,1,0:T(8,128)(2,1)S(1)}, u32[]{:S(2)}) copy-start(bf16[8,32,1024]{2,1,0:T(8,128)(2,1)S(1)} %all_to_all.25.up_hbm) | copy-start | bytes 1572868
  36.9 22.4 %all-to-all-start.1 = ((f32[8,32,1024]{2,1,0:T(8,128)}), f32[8,32,1024]{2,1,0:T(8,128)S(1)}, u32[]{:S(2)}, u32[]{:S(2)}) async-start(f32[8,32,1024]{2,1,0:T(8,128)} %broadcast_in_dim.2), calls=%async_computation.1 | async-start | bytes 2097152 | tf_op jit(solution)/shard_map/all_to_all | solution.py:597
  41.3 4.1 %collective-permute-start.1 = (bf16[8,32,1024]{2,1,0:T(8,128)(2,1)S(1)}, bf16[8,32,1024]{2,1,0:T(8,128)(2,1)S(1)}, u32[]{:S(2)}, u32[]{:S(2)}) collective-permute-start(bf16[8,32,1024]{2,1,0:T(8,128)(2,1)S(1)} %all_to_all.25.up_hbm), channel_id=1, source_target_pairs={{0,1},{1,0},{2,3},{3,2},{4,5},{5,4},{6,7},{7,6},{8,9},{9,8},{10,11... | collective-permute-start | bytes 1572872 | tf_op jit(solution)/shard_map/ppermute | solution.py:46
  59.2 9.3 %copy-start = (f32[512,1024]{1,0:T(8,128)S(1)}, f32[512,1024]{1,0:T(8,128)}, u32[]{:S(2)}) copy-start(f32[512,1024]{1,0:T(8,128)} %m_ref.1) | copy-start | bytes 6291460
  59.2 9.3 %copy-start.3 = (s32[3]{0:T(128)S(1)}, s32[3]{0:T(128)}, u32[]{:S(2)}) copy-start(s32[3]{0:T(128)} %pad_add_fusion.s_ref) | copy-start | bytes 40
  59.2 63.3 %all-to-all-start.2 = ((bf16[4,8,512,128]{3,2,1,0:T(8,128)(2,1)}), bf16[4,8,512,128]{3,2,1,0:T(8,128)(2,1)}, u32[]{:S(2)}, u32[]{:S(2)}) async-start(bf16[4,8,512,128]{3,2,1,0:T(8,128)(2,1)} %get-tuple-element.64), calls=%async_computation.2 | async-start | bytes 8388608 | tf_op jit(solution)/shard_map/all_to_all | solution.py:597
  64.2 4.3 %collective-permute-start.2 = (f32[8,32,1024]{2,1,0:T(8,128)S(1)}, f32[8,32,1024]{2,1,0:T(8,128)S(1)}, u32[]{:S(2)}, u32[]{:S(2)}) collective-permute-start(f32[8,32,1024]{2,1,0:T(8,128)S(1)} %all-to-all-done.1.b_ref), channel_id=1, source_target_pairs={{0,1},{1,0},{2,3},{3,2},{4,5},{5,4},{6,7},{7,6},{8,9},{9,8},{10,11... | collective-permute-start | bytes 3145736 | tf_op jit(solution)/shard_map/ppermute | solution.py:46
  75.3 31.7 %collective-permute-start.3 = (bf16[512,1024]{1,0:T(8,128)(2,1)S(1)}, bf16[512,1024]{1,0:T(8,128)(2,1)}, u32[]{:S(2)}, u32[]{:S(2)}) collective-permute-start(bf16[512,1024]{1,0:T(8,128)(2,1)S(1)} %get-tuple-element.60.rest_0_), channel_id=1, source_target_pairs={{0,2},{1,7},{2,4},{3,1},{4,6},{5,3},{6,0},{7,5},{8,10},{9,15},{10,... | collective-permute-start | bytes 3145736 | tf_op jit(solution)/shard_map/ppermute | solution.py:46
  75.8 33.2 %collective-permute-start.4 = (bf16[512,1024]{1,0:T(8,128)(2,1)S(1)}, bf16[512,1024]{1,0:T(8,128)(2,1)S(1)}, u32[]{:S(2)}, u32[]{:S(2)}) collective-permute-start(bf16[512,1024]{1,0:T(8,128)(2,1)S(1)} %get-tuple-element.60.rest_0_), channel_id=1, source_target_pairs={{0,6},{1,3},{2,0},{3,5},{4,2},{5,7},{6,4},{7,1},{8,14},{9,11},{10,... | collective-permute-start | bytes 3145736 | tf_op jit(solution)/shard_map/ppermute | solution.py:46
  77.1 31.9 %collective-permute-start.5 = (bf16[512,1024]{1,0:T(8,128)(2,1)S(1)}, bf16[512,1024]{1,0:T(8,128)(2,1)}, u32[]{:S(2)}, u32[]{:S(2)}) collective-permute-start(bf16[512,1024]{1,0:T(8,128)(2,1)S(1)} %get-tuple-element.60.rest_0_), channel_id=1, source_target_pairs={{0,24},{1,25},{2,26},{3,27},{4,28},{5,29},{6,30},{7,31},{8,16},{9,... | collective-permute-start | bytes 3145736 | tf_op jit(solution)/shard_map/ppermute | solution.py:46
  110.0 37.5 %collective-permute-start.6 = (bf16[512,1024]{1,0:T(8,128)(2,1)}, bf16[512,1024]{1,0:T(8,128)(2,1)}, u32[]{:S(2)}, u32[]{:S(2)}) collective-permute-start(bf16[512,1024]{1,0:T(8,128)(2,1)} %collective-permute-done.3.rest_1_), channel_id=1, source_target_pairs={{0,2},{1,7},{2,4},{3,1},{4,6},{5,3},{6,0},{7,5},{8,10},{9,15},{10,... | collective-permute-start | bytes 3145736 | tf_op jit(solution)/shard_map/ppermute | solution.py:46
  110.4 37.1 %collective-permute-start.7 = (bf16[512,1024]{1,0:T(8,128)(2,1)}, bf16[512,1024]{1,0:T(8,128)(2,1)S(1)}, u32[]{:S(2)}, u32[]{:S(2)}) collective-permute-start(bf16[512,1024]{1,0:T(8,128)(2,1)} %collective-permute-done.5.rest_3_), channel_id=1, source_target_pairs={{0,6},{1,3},{2,0},{3,5},{4,2},{5,7},{6,4},{7,1},{8,14},{9,11},{10,... | collective-permute-start | bytes 3145736 | tf_op jit(solution)/shard_map/ppermute | solution.py:46
  111.4 36.1 %collective-permute-start.8 = (bf16[512,1024]{1,0:T(8,128)(2,1)}, bf16[512,1024]{1,0:T(8,128)(2,1)}, u32[]{:S(2)}, u32[]{:S(2)}) collective-permute-start(bf16[512,1024]{1,0:T(8,128)(2,1)} %collective-permute-done.3.rest_1_), channel_id=1, source_target_pairs={{0,24},{1,25},{2,26},{3,27},{4,28},{5,29},{6,30},{7,31},{8,16},{9,... | collective-permute-start | bytes 3145736 | tf_op jit(solution)/shard_map/ppermute | solution.py:46
  121.0 3.1 %collective-permute-start.9 = (bf16[320,512]{1,0:T(8,128)(2,1)}, bf16[320,512]{1,0:T(8,128)(2,1)S(1)}, u32[]{:S(2)}, u32[]{:S(2)}) collective-permute-start(bf16[320,512]{1,0:T(8,128)(2,1)} %low_rank.1.low_hbm), channel_id=1, source_target_pairs={{0,1},{1,0},{2,3},{3,2},{4,5},{5,4},{6,7},{7,6},{8,9},{9,8},{10,11... | collective-permute-start | bytes 983048 | tf_op jit(solution)/shard_map/ppermute | solution.py:46
  130.4 36.9 %all-to-all-start.3 = ((bf16[16,384,128]{2,1,0:T(8,128)(2,1)}), bf16[16,384,128]{2,1,0:T(8,128)(2,1)S(1)}, u32[]{:S(2)}, u32[]{:S(2)}) async-start(bf16[16,384,128]{2,1,0:T(8,128)(2,1)} %owner_pieces.1), calls=%async_computation.3 | async-start | bytes 3145728 | tf_op jit(solution)/shard_map/all_to_all | solution.py:597
  148.5 5.9 %collective-permute-start.12 = (bf16[320,2048]{1,0:T(8,128)(2,1)}, bf16[320,2048]{1,0:T(8,128)(2,1)S(1)}, u32[]{:S(2)}, u32[]{:S(2)}) collective-permute-start(bf16[320,2048]{1,0:T(8,128)(2,1)} %get-tuple-element.77), channel_id=1, source_target_pairs={{0,1},{1,0},{2,3},{3,2},{4,5},{5,4},{6,7},{7,6},{8,9},{9,8},{10,11... | collective-permute-start | bytes 3932168 | tf_op jit(solution)/shard_map/ppermute | solution.py:46
  151.5 22.6 %collective-permute-start.10 = (bf16[512,1024]{1,0:T(8,128)(2,1)}, bf16[512,1024]{1,0:T(8,128)(2,1)}, u32[]{:S(2)}, u32[]{:S(2)}) collective-permute-start(bf16[512,1024]{1,0:T(8,128)(2,1)} %copy-done.7), channel_id=1, source_target_pairs={{0,6},{1,3},{2,0},{3,5},{4,2},{5,7},{6,4},{7,1},{8,14},{9,11},{10,... | collective-permute-start | bytes 3145736 | tf_op jit(solution)/shard_map/ppermute | solution.py:46
  168.8 28.1 %all-to-all-start.4 = ((f32[8,192,256]{2,1,0:T(8,128)}), f32[8,192,256]{2,1,0:T(8,128)S(1)}, u32[]{:S(2)}, u32[]{:S(2)}) async-start(f32[8,192,256]{2,1,0:T(8,128)} %sum_pieces.1), calls=%async_computation.4 | async-start | bytes 3145728 | tf_op jit(solution)/shard_map/all_to_all | solution.py:597
  173.5 6.6 %collective-permute-start.13 = (f32[320,1024]{1,0:T(8,128)}, f32[320,1024]{1,0:T(8,128)S(1)}, u32[]{:S(2)}, u32[]{:S(2)}) collective-permute-start(f32[320,1024]{1,0:T(8,128)} %get-tuple-element.84), channel_id=1, source_target_pairs={{0,1},{1,0},{2,3},{3,2},{4,5},{5,4},{6,7},{7,6},{8,9},{9,8},{10,11... | collective-permute-start | bytes 3932168 | tf_op jit(solution)/shard_map/ppermute | solution.py:46
  174.2 4.5 %collective-permute-start.11 = (bf16[512,1024]{1,0:T(8,128)(2,1)}, bf16[512,1024]{1,0:T(8,128)(2,1)}, u32[]{:S(2)}, u32[]{:S(2)}) collective-permute-start(bf16[512,1024]{1,0:T(8,128)(2,1)} %collective-permute-done.10.w_hbm), channel_id=1, source_target_pairs={{0,1},{1,0},{2,3},{3,2},{4,5},{5,4},{6,7},{7,6},{8,9},{9,8},{10,11... | collective-permute-start | bytes 3145736 | tf_op jit(solution)/shard_map/ppermute | solution.py:46
  174.2 5.8 %collective-permute-start.14 = (bf16[320,1536]{1,0:T(8,128)(2,1)}, bf16[320,1536]{1,0:T(8,128)(2,1)}, u32[]{:S(2)}, u32[]{:S(2)}) collective-permute-start(bf16[320,1536]{1,0:T(8,128)(2,1)} %get-tuple-element.86), channel_id=1, source_target_pairs={{0,1},{1,0},{2,3},{3,2},{4,5},{5,4},{6,7},{7,6},{8,9},{9,8},{10,11... | collective-permute-start | bytes 2949128 | tf_op jit(solution)/shard_map/ppermute | solution.py:46
  (9 other events, 14.1 us)
Sparse Core Ops, SparseCore 0:
  10.4 89.2 all-gather.1

commit v2 on v1

--- a/solution.py
+++ b/solution.py
@@ -370,7 +370,7 @@
         ins.append(
             [
                 pltpu.make_async_copy(w_hbm[u], wbuf.at[span(u)], wsems.at[0, u]),
-                pltpu.make_async_copy(d_hbm.at[column(s_ref[u])], dbuf.at[u], wsems.at[1, u]),
+                pltpu.make_async_copy(d_hbm.at[column(s_ref[2 * units + before + u])], dbuf.at[u], wsems.at[1, u]),
             ]
         )
         here = t_hbm.at[:, column(s_ref[u])]
@@ -462,8 +462,8 @@
     total = in_ref[0].astype(f32)
     for k in range(1, 16):
         total = total + in_ref[k].astype(f32)
-    down = total[:256].T
-    up = total[256:]
+    down = total[:256].T.astype(bf16)
+    up = total[256:].astype(bf16)
     for k in range(8):
         o_ref[k, :128] = down
         for j in range(2):
@@ -477,7 +477,7 @@
         sum_kernel,
         in_specs=[vm],
         out_specs=vm,
-        out_shape=jax.ShapeDtypeStruct((8, 192, 256), f32),
+        out_shape=jax.ShapeDtypeStruct((8, 192, 256), bf16),
         compiler_params=pltpu.CompilerParams(vmem_limit_bytes=VMEM),
         cost_estimate=COST,
         name="sum_pieces",
@@ -487,11 +487,13 @@
 def join_kernel(in_ref, down_ref, up_ref):
     for y in range(4):
         for zl in range(2):
-            down_ref[128 * y : 128 * y + 128, 256 * zl : 256 * zl + 256] = in_ref[2 * y + zl, :128]
+            there = slice(256 * zl, 256 * zl + 256)
+            down_ref[128 * y : 128 * y + 128, there] = in_ref[2 * y + zl, :128].astype(f32)
     for zl in range(2):
         for j in range(2):
             rows = slice(128 + 32 * j, 160 + 32 * j)
-            total = in_ref[zl, rows] + in_ref[2 + zl, rows] + in_ref[4 + zl, rows] + in_ref[6 + zl, rows]
+            parts = [in_ref[2 * y + zl, rows].astype(f32) for y in range(4)]
+            total = (parts[0] + parts[1]) + (parts[2] + parts[3])
             up_ref[:, 512 * zl + 256 * j : 512 * zl + 256 * j + 256] = total
 
 
@@ -508,19 +510,57 @@
     )(pieces)
 
 
+def place_kernel(s_ref, r_hbm, vo_hbm, vr_hbm, low_hbm, up_hbm, x_in, v_hbm, x_hbm, rbuf, vo, vr, low, up, sems, xsems, vsems):
+    ins = start([pltpu.make_async_copy(low_hbm, low, sems.at[0]), pltpu.make_async_copy(up_hbm, up, sems.at[1])])
+    late = start([pltpu.make_async_copy(r_hbm, rbuf, sems.at[2])])
+    ins += start([pltpu.make_async_copy(vo_hbm, vo, sems.at[3]), pltpu.make_async_copy(vr_hbm, vr, sems.at[4])])
+    wait(late)
+    outs = []
+    for u in range(4):
+        there = x_hbm.at[:, column(s_ref[u])]
+        outs += start([pltpu.make_async_copy(rbuf.at[:, pl.ds(512 * u, 512)], there, xsems.at[u])])
+    wait(ins)
+    for j in range(4):
+        cols = slice(256 * j, 256 * j + 256)
+        there = pl.ds(256 * j, 256)
+        vo[:, cols] = vo[:, cols] + vr[:, cols] + scale * nn(low[...], up[:, cols])
+        outs += start([pltpu.make_async_copy(vo.at[:, there], v_hbm.at[:, there], vsems.at[j])])
+    wait(outs)
+
+
+def place_columns(x, recv, vo, vr, low, up, starts):
+    n, d = x.shape
+    return call(
+        place_kernel,
+        "place_columns",
+        (starts, recv, vo, vr, low, up, x),
+        [((n, 1024), f32), ((n, d), bf16)],
+        [
+            pltpu.VMEM((n, 2048), bf16),
+            pltpu.VMEM((n, 1024), f32),
+            pltpu.VMEM((n, 1024), f32),
+            pltpu.VMEM((n, 512), bf16),
+            pltpu.VMEM((512, 1024), bf16),
+            pltpu.SemaphoreType.DMA((5,)),
+            pltpu.SemaphoreType.DMA((4,)),
+            pltpu.SemaphoreType.DMA((4,)),
+        ],
+        {6: 1},
+    )
+
+
 def finish_kernel(
-    s_ref, t_hbm, d_hbm, w_hbm, ws_hbm, cot_hbm, br_hbm, vo_hbm, vr_hbm, low_hbm, up_hbm, r_hbm, x_in,
-    v_hbm, x_hbm, tbuf, wbuf, dbuf, xbuf, cot, br, vo, vr, low, up, vbuf, lbuf, sems, wsems, xsems, vsems,
+    s_ref, t_hbm, d_hbm, w_hbm, ws_hbm, cot_hbm, br_hbm, vs_hbm, x_in,
+    v_hbm, x_hbm, tbuf, wbuf, dbuf, xbuf, cot, br, vs, vbuf, sems, wsems, xsems, vsems,
 ):
     n = cot.shape[0]
-    late = [pltpu.make_async_copy(r_hbm, lbuf, sems.at[0])]
     first = start(
         [
             pltpu.make_async_copy(cot_hbm, cot, sems.at[1]),
             pltpu.make_async_copy(br_hbm.at[pl.ds(0, n)], br, sems.at[2]),
         ]
     )
-    ins, tokens = [], []
+    ins, rest = [], []
     for i, w in enumerate((w_hbm, ws_hbm)):
         there = pl.ds(512 * i, 512)
         ins.append(
@@ -529,42 +569,32 @@
                 pltpu.make_async_copy(d_hbm.at[column(s_ref[i])], dbuf.at[i], wsems.at[1, i]),
             ]
         )
-        tokens.append(pltpu.make_async_copy(t_hbm.at[:, column(s_ref[i])], tbuf.at[:, there], wsems.at[2, i]))
-    rest = tokens + [
-        pltpu.make_async_copy(low_hbm, low, sems.at[3]),
-        pltpu.make_async_copy(up_hbm, up, sems.at[4]),
-        pltpu.make_async_copy(vo_hbm, vo, sems.at[5]),
-        pltpu.make_async_copy(vr_hbm, vr, sems.at[6]),
-    ]
+        rest.append(pltpu.make_async_copy(t_hbm.at[:, column(s_ref[i])], tbuf.at[:, there], wsems.at[2, i]))
+    rest.append(pltpu.make_async_copy(vs_hbm, vs, sems.at[0]))
     start(ins[0])
     wait(first)
     outs = []
     for i in range(2):
         wait(ins[i])
-        start(late + ins[1] if i == 0 else rest)
+        start(ins[1] if i == 0 else rest)
         x = nt(cot[...], wbuf[512 * i : 512 * i + 512, :]) + scale * nt(br[...], dbuf[i])
         xbuf[i] = x.astype(bf16)
         outs += start([pltpu.make_async_copy(xbuf.at[i], x_hbm.at[:, column(s_ref[i])], xsems.at[i])])
-    wait(late)
-    for u in range(3):
-        there = x_hbm.at[:, column(s_ref[2 + u])]
-        outs += start([pltpu.make_async_copy(lbuf.at[:, pl.ds(512 * u, 512)], there, xsems.at[2 + u])])
     wait(rest)
     for j in range(4):
         cols = slice(256 * j, 256 * j + 256)
         there = pl.ds(256 * j, 256)
-        v = nn(tbuf[...], wbuf[:, cols]) + scale * nn(low[...], up[:, cols])
-        vbuf[:, cols] = (vo[:, cols] + vr[:, cols] + v).astype(bf16)
+        vbuf[:, cols] = (vs[:, cols] + nn(tbuf[...], wbuf[:, cols])).astype(bf16)
         outs += start([pltpu.make_async_copy(vbuf.at[:, there], v_hbm.at[:, there], vsems.at[j])])
     wait(outs)
 
 
-def finish(x, recv, tokens, down, w, w_sib, cot, br2, vo, vr, low, up, starts):
+def finish(x, tokens, down, w, w_sib, cot, br2, vs, starts):
     n, d = x.shape
     return call(
         finish_kernel,
         "finish",
-        (starts, tokens, down, w, w_sib, cot, br2, vo, vr, low, up, recv, x),
+        (starts, tokens, down, w, w_sib, cot, br2, vs, x),
         [((n, 1024), bf16), ((n, d), bf16)],
         [
             pltpu.VMEM((n, 1024), bf16),
@@ -574,17 +604,13 @@
             pltpu.VMEM((n, 1024), bf16),
             pltpu.VMEM((n, 512), bf16),
             pltpu.VMEM((n, 1024), f32),
-            pltpu.VMEM((n, 1024), f32),
-            pltpu.VMEM((n, 512), bf16),
-            pltpu.VMEM((512, 1024), bf16),
             pltpu.VMEM((n, 1024), bf16),
-            pltpu.VMEM((n, 1536), bf16),
-            pltpu.SemaphoreType.DMA((7,)),
+            pltpu.SemaphoreType.DMA((3,)),
             pltpu.SemaphoreType.DMA((3, 2)),
-            pltpu.SemaphoreType.DMA((5,)),
+            pltpu.SemaphoreType.DMA((2,)),
             pltpu.SemaphoreType.DMA((4,)),
         ],
-        {12: 1},
+        {8: 1},
     )
 
 
@@ -612,9 +638,10 @@
     copies, down_half, place = bar((copies, down_half, place))
     up = to_owners(copies, ("zh", "x"))
     down = lax.all_gather(down_half, ("zh", "x", "c"), axis=0, tiled=True)
-    tokens_sib = send(pick_columns(tokens, cot, place), "core")
+    picked = pick_columns(tokens, cot, place)
     prior = jnp.broadcast_to(prev_up[None], (8,) + prev_up.shape)
-    up, prior, tokens_sib = bar((up, prior, tokens_sib))
+    up, prior, picked = bar((up, prior, picked))
+    tokens_sib = send(picked, "core")
     up_sib = send(up, "core")
 
     prior = to_owners(prior, ("zh", "x"))
@@ -624,44 +651,50 @@
     g = to_owners(g, ("y",))
 
     merged, w = merge(master, prev_down, prior, prior_sib, place)
-    p, q, far = bar(first_step(w))
-    second = second_step(p, q, far)
-
-    def blocks_of(core):
+    first = first_step(w)
+
+    def groups_of(core):
         s = 1 - 2 * core
         p, q, r = (x - s) % 4, (x + s) % 4, (x + 2) % 4
         here, there = 4 * zh, 4 * (1 - zh)
-        one = jnp.stack([here + x, here + p, here + q, there + x])
-        two = jnp.stack([here + r, there + p, there + q])
-        return one, two, (there + r)[None]
-
-    own = blocks_of(c)
-    sib = [2 * k + 1 - c for k in blocks_of(1 - c)]
+        own, two = (here + x)[None], jnp.stack([here + p, here + q])
+        four = jnp.stack([there + x, here + r, there + p, there + q])
+        return own, two, four, (there + r)[None]
+
+    own = groups_of(c)
+    mine = [2 * k + c for k in own]
+    sib = [2 * k + 1 - c for k in groups_of(1 - c)]
     starts = [
-        jnp.concatenate([2 * own[0] + c, own[0]]),
-        jnp.concatenate([2 * own[1] + c, own[1], sib[0]]),
-        jnp.concatenate([2 * own[2] + c, sib[2], sib[1]]),
+        jnp.concatenate([mine[0], own[0], 0 * own[0]]),
+        jnp.concatenate([mine[1], own[1], sib[0], mine[1]]),
+        jnp.concatenate([mine[2], own[2], sib[1], mine[2]]),
+        sib[2],
+        jnp.concatenate([mine[3], sib[3]]),
     ]
     starts = [v.astype(jnp.int32) for v in starts]
 
+    vo, vs, dx, other = main_group(tokens, tokens_sib, down_half, cot, br2, [w], starts[0])
+    p, q, far, vo, vs, dx, other = bar(first + (vo, vs, dx, other))
+    second = second_step(p, q, far)
+
+    shared = (tokens, tokens_sib, down, cot, br2)
     low = low_rank(tokens, down, place)
     pieces = owner_pieces(g, low, send(low, "core"), cot, tokens_sib, place)
-    shared = (tokens, tokens_sib, down, cot, br2)
     pieces, p = bar((pieces, p))
-    part = main_group(*shared, [w, p, q, far], starts[0])
+    part = main_group(*shared, [p, q], starts[1], 1, (vo, vs, dx, send(other, "core")))
     r, far_q, far_p, part = bar(second + (part,))
 
     far_r = send(far_q, "xq")
     pieces = to_owners(pieces, ("zh", "x", "zl"))
     vo, vs, dx, other = part
-    part = main_group(*shared, [r, far_p, far_q], starts[1], 4, (vo, vs, dx, send(other, "core")))
+    part = main_group(*shared, [far, r, far_p, far_q], starts[2], 2, (vo, vs, dx, send(other, "core")))
     part, pieces = bar((part, sum_pieces(pieces)))
 
     pieces = to_owners(pieces, ("y", "zl"))
     vo, vs, dx, other = part
-    values, dx = finish(
-        dx, send(other, "core"), tokens, down, far_r, send(far_r, "core"), cot, br2, vo, send(vs, "core"), low, up_rows, starts[2]
-    )
+    v, dx = place_columns(dx, send(other, "core"), vo, send(vs, "core"), low, up_rows, starts[3])
+    values, dx = finish(dx, tokens, down, far_r, send(far_r, "core"), cot, br2, v, starts[4])
+    pieces, values = bar((pieces, values))
     down_grad, up_grad = join_pieces(pieces)
     return merged, values, dx, down_grad, up_grad
 

time: 207 us -> 192 us (0.928)
  blocking collectives: 20.2 us -> 0 us
  Pallas kernels: 71.1 us -> 78.2 us
  waiting for transfers between devices: 48.1 us -> 44.5 us
  starting transfers between devices: 40.6 us -> 42.8 us
    all_to_all x1 -> x0, blocking collectives: 20.2 us -> none  [to_owners(): return lax.all_to_all(v, axes, split_axis=0, concat_axis=0)]
    all_to_all x4 -> x5, starting transfers between devices: 17.8 us -> 26.9 us  [to_owners(): return lax.all_to_all(v, axes, split_axis=0, concat_axis=0)]
    pallas_call x7 -> x9, Pallas kernels: 60.7 us -> 67.8 us  [call(): pl.pallas_call(kernel, in_specs=[pl.BlockSpec(memory_space=pltpu.SMEM)] +...]
    ppermute x15 -> x16, starting transfers between devices: 22.7 us -> 15.8 us  [send(): return lax.ppermute(v, AXES, MOVES[move])]
    ppermute x15 -> x16, waiting for transfers between devices: 39.1 us -> 33.7 us  [send(): return lax.ppermute(v, AXES, MOVES[move])]
    all_to_all x4 -> x5, waiting for transfers between devices: 8.96 us -> 10.8 us  [to_owners(): return lax.all_to_all(v, axes, split_axis=0, concat_axis=0)]
    unnamed x26 -> x28, local copies, waits for them, and re-layouts: 6.83 us -> 5.77 us
  transfers between devices with their start and end apart: 20 -> 22, of which waited for: 10 -> 10; matrix products, arithmetic and copies ran while one was open for 2% -> 2% of each run, Pallas kernels for 33% -> 39%
where the time goes in v2:
time: 192 us; the launch traced here: 191 us
  Pallas kernels  78.2 us (41%)
  waiting for transfers between devices  44.5 us (23%)
  starting transfers between devices  42.8 us (22%)
  between operations  14.3 us (7%)
  local copies, waits for them, and re-layouts  8.22 us (4%)
  other arithmetic  2.76 us (1%)
    pallas_call x9, Pallas kernels, call(): pl.pallas_call(kernel, in_specs=[pl.BlockSpec(memory_space=pltpu.SMEM)] +...  67.8 us
    ppermute x16, waiting for transfers between devices, send(): return lax.ppermute(v, AXES, MOVES[move])  33.7 us
    all_to_all x5, starting transfers between devices, to_owners(): return lax.all_to_all(v, axes, split_axis=0, concat_axis=0)  26.9 us
    ppermute x16, starting transfers between devices, send(): return lax.ppermute(v, AXES, MOVES[move])  15.8 us
    all_to_all x5, waiting for transfers between devices, to_owners(): return lax.all_to_all(v, axes, split_axis=0, concat_axis=0)  10.8 us
    pallas_call x1, Pallas kernels, merge(): pl.pallas_call(merge_kernel, grid=(1,), in_specs=[pl.BlockSpec(memory_spa...  5.84 us
    unnamed x28, local copies, waits for them, and re-layouts  5.77 us
  transfers between devices with their start and end apart: 22, of which 10 were waited for; matrix products, arithmetic and copies ran while one was open for 2% of the time, Pallas kernels for 39%

profile of v2, /device:TPU:1, one launch (start us, length us, event | category | flops | bytes accessed | tf_op | source)
XLA Modules:
  0.0 190.7 jit_solution(14993604875712970883)
XLA Ops:
  7.2 2.3 %prepare.1 = (bf16[8,32,1024]{2,1,0:T(8,128)(2,1)}, bf16[512,512]{1,0:T(8,128)(2,1)}) custom-call(f32[32,1024]{1,0:T(8,128)} %up_ref.1, f32[512,512]{1,0:T(8,128)} %down_ref.1), custom_call_target="tpu_custom_call" | custom-call | bytes 65536 | tf_op jit(solution)/shard_map/prepare/pallas_call | solution.py:118
  10.2 8.2 %all-to-all-start = ((bf16[8,32,1024]{2,1,0:T(8,128)(2,1)}), bf16[8,32,1024]{2,1,0:T(8,128)(2,1)S(1)}, u32[]{:S(2)}, u32[]{:S(2)}) async-start(bf16[8,32,1024]{2,1,0:T(8,128)(2,1)} %get-tuple-element.64), calls=%async_computation | async-start | bytes 1048576 | tf_op jit(solution)/shard_map/all_to_all | solution.py:623
  18.4 3.9 %pick_columns.1 = bf16[320,5120]{1,0:T(8,128)(2,1)} custom-call(s32[3]{0:T(128)} %pad_add_fusion.s_ref, bf16[320,8192]{1,0:T(8,128)(2,1)} %t_hbm.9, bf16[320,1024]{1,0:T(8,128)(2,1)} %cot_hbm.9), custom_call_target="tpu_custom_call" | custom-call | bytes 65536 | tf_op jit(solution)/shard_map/pick_columns/pallas_call | solution.py:63
  22.3 7.8 %all-to-all-done.up_hbm = bf16[8,32,1024]{2,1,0:T(8,128)(2,1)S(1)} async-done(((bf16[8,32,1024]{2,1,0:T(8,128)(2,1)}), bf16[8,32,1024]{2,1,0:T(8,128)(2,1)S(1)}, u32[]{:S(2)}, u32[]{:S(2)}) %all-to-all-start) | async-done | bytes 524320 | tf_op jit(solution)/shard_map/all_to_all | solution.py:623
  32.1 3.6 %all-to-all-start.1 = ((f32[8,32,1024]{2,1,0:T(8,128)}), f32[8,32,1024]{2,1,0:T(8,128)S(1)}, u32[]{:S(2)}, u32[]{:S(2)}) async-start(f32[8,32,1024]{2,1,0:T(8,128)} %broadcast_in_dim.4), calls=%async_computation.1 | async-start | bytes 2097152 | tf_op jit(solution)/shard_map/all_to_all | solution.py:623
  35.8 2.6 %collective-permute-done.1.ups_hbm = bf16[8,32,1024]{2,1,0:T(8,128)(2,1)S(1)} collective-permute-done((bf16[8,32,1024]{2,1,0:T(8,128)(2,1)S(1)}, bf16[8,32,1024]{2,1,0:T(8,128)(2,1)S(1)}, u32[]{:S(2)}, u32[]{:S(2)}) %collective-permute-start.1) | collective-permute-done | bytes 524320 | tf_op jit(solution)/shard_map/ppermute | solution.py:46
  39.1 10.9 %rank_partials.1 = (bf16[4,8,512,128]{3,2,1,0:T(8,128)(2,1)}, bf16[512,1024]{1,0:T(8,128)(2,1)}, bf16[640,512]{1,0:T(8,128)(2,1)}) custom-call(s32[3]{0:T(128)} %pad_add_fusion.s_ref, bf16[320,8192]{1,0:T(8,128)(2,1)} %t_hbm.9, bf16[320,5120]{1,0:T(8,128)(2,1)} %collective-permute-done.tr_hbm.refs_2_, bf16[320,1024]{1,0:T(8,128)(2,1)} %cot_hbm.9, ...), custom_call_target="tpu_custom_call" | custom-call | bytes 65536 | tf_op jit(solution)/shard_map/rank_partials/pallas_call | solution.py:63
  50.1 3.0 %all-to-all-done.1.b_ref = f32[8,32,1024]{2,1,0:T(8,128)S(1)} async-done(((f32[8,32,1024]{2,1,0:T(8,128)}), f32[8,32,1024]{2,1,0:T(8,128)S(1)}, u32[]{:S(2)}, u32[]{:S(2)}) %all-to-all-start.1) | async-done | bytes 1048608 | tf_op jit(solution)/shard_map/all_to_all | solution.py:623
  53.1 5.2 %all-to-all-start.2 = ((bf16[4,8,512,128]{3,2,1,0:T(8,128)(2,1)}), bf16[4,8,512,128]{3,2,1,0:T(8,128)(2,1)}, u32[]{:S(2)}, u32[]{:S(2)}) async-start(bf16[4,8,512,128]{3,2,1,0:T(8,128)(2,1)} %get-tuple-element.80), calls=%async_computation.2 | async-start | bytes 8388608 | tf_op jit(solution)/shard_map/all_to_all | solution.py:623
  58.9 2.3 %collective-permute-done.2.bs_ref = f32[8,32,1024]{2,1,0:T(8,128)S(1)} collective-permute-done((f32[8,32,1024]{2,1,0:T(8,128)S(1)}, f32[8,32,1024]{2,1,0:T(8,128)S(1)}, u32[]{:S(2)}, u32[]{:S(2)}) %collective-permute-start.2) | collective-permute-done | bytes 1048608 | tf_op jit(solution)/shard_map/ppermute | solution.py:46
  62.4 5.8 %merge.1 = (f32[512,1024]{1,0:T(8,128)}, bf16[512,1024]{1,0:T(8,128)(2,1)}) custom-call(s32[3]{0:T(128)S(1)} %copy-done.2, f32[512,1024]{1,0:T(8,128)S(1)} %copy-done, f32[512,512]{1,0:T(8,128)S(1)} %copy-done.1, f32[8,32,1024]{2,1,0:T(8,128)S(1)} %all-to-all-done.1.b_ref, f32[8,32,1024]{2,1,0:T(8,128)S(1)} %collective-permute-done.2.bs_ref), custom_call_target="tpu_custom_call" | custom-call | bytes 65536 | tf_op jit(solution)/shard_map/merge/pallas_call | solution.py:335
  68.3 2.2 %collective-permute-start.5 = (bf16[512,1024]{1,0:T(8,128)(2,1)}, bf16[512,1024]{1,0:T(8,128)(2,1)S(1)}, u32[]{:S(2)}, u32[]{:S(2)}) collective-permute-start(bf16[512,1024]{1,0:T(8,128)(2,1)} %get-tuple-element.73.rest_0_), channel_id=1, source_target_pairs={{0,24},{1,25},{2,26},{3,27},{4,28},{5,29},{6,30},{7,31},{8,16},{9,... | collective-permute-start | bytes 3145736 | tf_op jit(solution)/shard_map/ppermute | solution.py:46
  73.8 6.0 %main_group.3 = (f32[320,1024]{1,0:T(8,128)}, f32[320,1024]{1,0:T(8,128)}, bf16[320,8192]{1,0:T(8,128)(2,1)}, bf16[320,512]{1,0:T(8,128)(2,1)}) custom-call(s32[3]{0:T(128)} %pad_add_fusion.2.s_ref, bf16[320,8192]{1,0:T(8,128)(2,1)} %t_hbm.9, bf16[320,5120]{1,0:T(8,128)(2,1)} %collective-permute-done.tr_hbm.refs_2_, ...), custom_call_target="tpu_custom_call" | custom-call | bytes 65536 | tf_op jit(solution)/shard_map/main_group/pallas_call | solution.py:63
  79.8 23.8 %collective-permute-done.5.refs_6_ = bf16[512,1024]{1,0:T(8,128)(2,1)S(1)} collective-permute-done((bf16[512,1024]{1,0:T(8,128)(2,1)}, bf16[512,1024]{1,0:T(8,128)(2,1)S(1)}, u32[]{:S(2)}, u32[]{:S(2)}) %collective-permute-start.5) | collective-permute-done | bytes 1048608 | tf_op jit(solution)/shard_map/ppermute | solution.py:46
  108.6 7.0 %low_rank.1.low_hbm = bf16[320,512]{1,0:T(8,128)(2,1)} custom-call(s32[3]{0:T(128)} %pad_add_fusion.s_ref, bf16[320,8192]{1,0:T(8,128)(2,1)} %t_hbm.9, bf16[8192,512]{1,0:T(8,128)(2,1)} %all-gather.2.cloned.1.call-done.d_hbm.refs_3_), custom_call_target="tpu_custom_call" | custom-call | bytes 65536 | tf_op jit(solution)/shard_map/low_rank/pallas_call | solution.py:63
  118.9 5.7 %owner_pieces.1 = bf16[16,384,128]{2,1,0:T(8,128)(2,1)} custom-call(s32[3]{0:T(128)} %pad_add_fusion.s_ref, bf16[4,8,512,128]{3,2,1,0:T(8,128)(2,1)} %all-to-all-done.2.g_hbm, bf16[320,512]{1,0:T(8,128)(2,1)} %low_rank.1.low_hbm, bf16[320,512]{1,0:T(8,128)(2,1)} %copy-done.11, bf16[320,1024]{1,0:T(8,128)(2,1)} %cot_hbm.9, ...), custom_call_target="tpu_custom_call" | custom-call | bytes 65536 | tf_op jit(solution)/shard_map/owner_pieces/pallas_call | solution.py:63
  124.6 4.9 %all-to-all-start.3 = ((bf16[16,384,128]{2,1,0:T(8,128)(2,1)}), bf16[16,384,128]{2,1,0:T(8,128)(2,1)S(1)}, u32[]{:S(2)}, u32[]{:S(2)}) async-start(bf16[16,384,128]{2,1,0:T(8,128)(2,1)} %owner_pieces.1), calls=%async_computation.3 | async-start | bytes 3145728 | tf_op jit(solution)/shard_map/all_to_all | solution.py:623
  132.2 9.1 %main_group.4 = (f32[320,1024]{1,0:T(8,128)}, f32[320,1024]{1,0:T(8,128)}, bf16[320,8192]{1,0:T(8,128)(2,1)}, bf16[320,1024]{1,0:T(8,128)(2,1)}) custom-call(s32[7]{0:T(128)} %concatenate.16.refs_0_, bf16[320,8192]{1,0:T(8,128)(2,1)} %t_hbm.9, bf16[320,5120]{1,0:T(8,128)(2,1)} %collective-permute-done.tr_hbm.refs_2_, ...), custom_call_target="tpu_custom_call", output_to_operand_aliasing={{2}: (10, {})} | custom-call | bytes 65536 | tf_op jit(solution)/shard_map/main_group/pallas_call | solution.py:63
  141.4 1.7 collective-permute-start.12
  143.1 1.9 collective-permute-start.11
  147.7 13.5 %main_group.5 = (f32[320,1024]{1,0:T(8,128)}, f32[320,1024]{1,0:T(8,128)}, bf16[320,8192]{1,0:T(8,128)(2,1)}, bf16[320,2048]{1,0:T(8,128)(2,1)}) custom-call(s32[14]{0:T(128)} %concatenate.14.refs_0_, bf16[320,8192]{1,0:T(8,128)(2,1)} %t_hbm.9, bf16[320,5120]{1,0:T(8,128)(2,1)} %collective-permute-done.tr_hbm.refs_2_, ...), custom_call_target="tpu_custom_call", output_to_operand_aliasing={{2}: (12, {})} | custom-call | bytes 65536 | tf_op jit(solution)/shard_map/main_group/pallas_call | solution.py:63
  163.3 5.1 %all-to-all-start.4 = ((bf16[8,192,256]{2,1,0:T(8,128)(2,1)}), bf16[8,192,256]{2,1,0:T(8,128)(2,1)S(1)}, u32[]{:S(2)}, u32[]{:S(2)}) async-start(bf16[8,192,256]{2,1,0:T(8,128)(2,1)} %sum_pieces.1), calls=%async_computation.4 | async-start | bytes 1572864 | tf_op jit(solution)/shard_map/all_to_all | solution.py:623
  171.1 4.8 %place_columns.1 = (f32[320,1024]{1,0:T(8,128)}, bf16[320,8192]{1,0:T(8,128)(2,1)}) custom-call(s32[4]{0:T(128)} %fusion.5.s_ref, bf16[320,2048]{1,0:T(8,128)(2,1)} %copy-done.4, f32[320,1024]{1,0:T(8,128)} %get-tuple-element.105.vo_hbm, f32[320,1024]{1,0:T(8,128)} %copy-done.5, bf16[320,512]{1,0:T(8,128)(2,1)} %low_rank.1.low_hbm, ...), custom_call_target="tpu_custom_call", output_to_operand_aliasing={{1}: (6, {})} | custom-call | bytes 65536 | tf_op jit(solution)/shard_map/place_columns/pallas_call | solution.py:63
  175.9 6.9 %finish.1 = (bf16[320,1024]{1,0:T(8,128)(2,1)}, bf16[320,8192]{1,0:T(8,128)(2,1)}) custom-call(s32[2]{0:T(128)} %pad_add_fusion.3.s_ref, bf16[320,8192]{1,0:T(8,128)(2,1)} %t_hbm.9, bf16[8192,512]{1,0:T(8,128)(2,1)} %all-gather.2.cloned.1.call-done.d_hbm.refs_3_, bf16[512,1024]{1,0:T(8,128)(2,1)} %collective-permute-done.12.w_hbm, ...), custom_call_target="tpu_custom_call", output_to_operand_aliasing={{1}: (8, {})} | custom-call | bytes 65536 | tf_op jit(solution)/shard_map/finish/pallas_call | solution.py:63
  (72 shorter events, 28.4 us)
Async XLA Ops:
  7.2 101.4 %all-gather.2.cloned.1.call-start = ((), (), s32[]{:S(2)}) async-start(), calls=%async_computation.5 | async-start | bytes 8912896 | tf_op jit(solution)/shard_map/all_gather | solution.py:640
  10.2 19.9 %all-to-all-start = ((bf16[8,32,1024]{2,1,0:T(8,128)(2,1)}), bf16[8,32,1024]{2,1,0:T(8,128)(2,1)S(1)}, u32[]{:S(2)}, u32[]{:S(2)}) async-start(bf16[8,32,1024]{2,1,0:T(8,128)(2,1)} %get-tuple-element.64), calls=%async_computation | async-start | bytes 1048576 | tf_op jit(solution)/shard_map/all_to_all | solution.py:623
  18.4 11.7 %copy-start.12 = (f32[32,1024]{1,0:T(8,128)S(1)}, f32[32,1024]{1,0:T(8,128)}, u32[]{:S(2)}) copy-start(f32[32,1024]{1,0:T(8,128)} %param.10) | copy-start | bytes 393220
  31.3 7.1 %collective-permute-start = (bf16[320,5120]{1,0:T(8,128)(2,1)}, bf16[320,5120]{1,0:T(8,128)(2,1)}, u32[]{:S(2)}, u32[]{:S(2)}) collective-permute-start(bf16[320,5120]{1,0:T(8,128)(2,1)} %pick_columns.1), channel_id=1, source_target_pairs={{0,1},{1,0},{2,3},{3,2},{4,5},{5,4},{6,7},{7,6},{8,9},{9,8},{10,11... | collective-permute-start | bytes 9830408 | tf_op jit(solution)/shard_map/ppermute | solution.py:46
  32.1 21.0 %all-to-all-start.1 = ((f32[8,32,1024]{2,1,0:T(8,128)}), f32[8,32,1024]{2,1,0:T(8,128)S(1)}, u32[]{:S(2)}, u32[]{:S(2)}) async-start(f32[8,32,1024]{2,1,0:T(8,128)} %broadcast_in_dim.4), calls=%async_computation.1 | async-start | bytes 2097152 | tf_op jit(solution)/shard_map/all_to_all | solution.py:623
  35.7 2.7 %collective-permute-start.1 = (bf16[8,32,1024]{2,1,0:T(8,128)(2,1)S(1)}, bf16[8,32,1024]{2,1,0:T(8,128)(2,1)S(1)}, u32[]{:S(2)}, u32[]{:S(2)}) collective-permute-start(bf16[8,32,1024]{2,1,0:T(8,128)(2,1)S(1)} %all-to-all-done.up_hbm), channel_id=1, source_target_pairs={{0,1},{1,0},{2,3},{3,2},{4,5},{5,4},{6,7},{7,6},{8,9},{9,8},{10,11... | collective-permute-start | bytes 1572872 | tf_op jit(solution)/shard_map/ppermute | solution.py:46
  53.1 63.6 %all-to-all-start.2 = ((bf16[4,8,512,128]{3,2,1,0:T(8,128)(2,1)}), bf16[4,8,512,128]{3,2,1,0:T(8,128)(2,1)}, u32[]{:S(2)}, u32[]{:S(2)}) async-start(bf16[4,8,512,128]{3,2,1,0:T(8,128)(2,1)} %get-tuple-element.80), calls=%async_computation.2 | async-start | bytes 8388608 | tf_op jit(solution)/shard_map/all_to_all | solution.py:623
  58.3 2.9 %collective-permute-start.2 = (f32[8,32,1024]{2,1,0:T(8,128)S(1)}, f32[8,32,1024]{2,1,0:T(8,128)S(1)}, u32[]{:S(2)}, u32[]{:S(2)}) collective-permute-start(f32[8,32,1024]{2,1,0:T(8,128)S(1)} %all-to-all-done.1.b_ref), channel_id=1, source_target_pairs={{0,1},{1,0},{2,3},{3,2},{4,5},{5,4},{6,7},{7,6},{8,9},{9,8},{10,11... | collective-permute-start | bytes 3145736 | tf_op jit(solution)/shard_map/ppermute | solution.py:46
  68.3 35.3 %collective-permute-start.5 = (bf16[512,1024]{1,0:T(8,128)(2,1)}, bf16[512,1024]{1,0:T(8,128)(2,1)S(1)}, u32[]{:S(2)}, u32[]{:S(2)}) collective-permute-start(bf16[512,1024]{1,0:T(8,128)(2,1)} %get-tuple-element.73.rest_0_), channel_id=1, source_target_pairs={{0,24},{1,25},{2,26},{3,27},{4,28},{5,29},{6,30},{7,31},{8,16},{9,... | collective-permute-start | bytes 3145736 | tf_op jit(solution)/shard_map/ppermute | solution.py:46
  70.4 34.3 %collective-permute-start.4 = (bf16[512,1024]{1,0:T(8,128)(2,1)}, bf16[512,1024]{1,0:T(8,128)(2,1)S(1)}, u32[]{:S(2)}, u32[]{:S(2)}) collective-permute-start(bf16[512,1024]{1,0:T(8,128)(2,1)} %get-tuple-element.73.rest_0_), channel_id=1, source_target_pairs={{0,6},{1,3},{2,0},{3,5},{4,2},{5,7},{6,4},{7,1},{8,14},{9,11},{10,... | collective-permute-start | bytes 3145736 | tf_op jit(solution)/shard_map/ppermute | solution.py:46
  71.7 33.8 %collective-permute-start.3 = (bf16[512,1024]{1,0:T(8,128)(2,1)}, bf16[512,1024]{1,0:T(8,128)(2,1)}, u32[]{:S(2)}, u32[]{:S(2)}) collective-permute-start(bf16[512,1024]{1,0:T(8,128)(2,1)} %get-tuple-element.73.rest_0_), channel_id=1, source_target_pairs={{0,2},{1,7},{2,4},{3,1},{4,6},{5,3},{6,0},{7,5},{8,10},{9,15},{10,... | collective-permute-start | bytes 3145736 | tf_op jit(solution)/shard_map/ppermute | solution.py:46
  103.6 11.9 %copy-start.6 = (bf16[512,1024]{1,0:T(8,128)(2,1)}, bf16[512,1024]{1,0:T(8,128)(2,1)S(1)}, u32[]{:S(2)}) copy-start(bf16[512,1024]{1,0:T(8,128)(2,1)S(1)} %collective-permute-done.5.refs_6_) | copy-start | bytes 3145732
  105.5 35.8 %collective-permute-start.7 = (bf16[512,1024]{1,0:T(8,128)(2,1)S(1)}, bf16[512,1024]{1,0:T(8,128)(2,1)}, u32[]{:S(2)}, u32[]{:S(2)}) collective-permute-start(bf16[512,1024]{1,0:T(8,128)(2,1)S(1)} %collective-permute-done.5.refs_6_), channel_id=1, source_target_pairs={{0,6},{1,3},{2,0},{3,5},{4,2},{5,7},{6,4},{7,1},{8,14},{9,11},{10,... | collective-permute-start | bytes 3145736 | tf_op jit(solution)/shard_map/ppermute | solution.py:46
  105.8 35.6 %collective-permute-start.8 = (bf16[512,1024]{1,0:T(8,128)(2,1)}, bf16[512,1024]{1,0:T(8,128)(2,1)}, u32[]{:S(2)}, u32[]{:S(2)}) collective-permute-start(bf16[512,1024]{1,0:T(8,128)(2,1)} %collective-permute-done.3.refs_6_), channel_id=1, source_target_pairs={{0,24},{1,25},{2,26},{3,27},{4,28},{5,29},{6,30},{7,31},{8,16},{9,... | collective-permute-start | bytes 3145736 | tf_op jit(solution)/shard_map/ppermute | solution.py:46
  107.2 34.2 %collective-permute-start.6 = (bf16[512,1024]{1,0:T(8,128)(2,1)}, bf16[512,1024]{1,0:T(8,128)(2,1)}, u32[]{:S(2)}, u32[]{:S(2)}) collective-permute-start(bf16[512,1024]{1,0:T(8,128)(2,1)} %collective-permute-done.3.refs_6_), channel_id=1, source_target_pairs={{0,2},{1,7},{2,4},{3,1},{4,6},{5,3},{6,0},{7,5},{8,10},{9,15},{10,... | collective-permute-start | bytes 3145736 | tf_op jit(solution)/shard_map/ppermute | solution.py:46
  115.6 2.6 %collective-permute-start.9 = (bf16[320,512]{1,0:T(8,128)(2,1)}, bf16[320,512]{1,0:T(8,128)(2,1)S(1)}, u32[]{:S(2)}, u32[]{:S(2)}) collective-permute-start(bf16[320,512]{1,0:T(8,128)(2,1)} %low_rank.1.low_hbm), channel_id=1, source_target_pairs={{0,1},{1,0},{2,3},{3,2},{4,5},{5,4},{6,7},{7,6},{8,9},{9,8},{10,11... | collective-permute-start | bytes 983048 | tf_op jit(solution)/shard_map/ppermute | solution.py:46
  124.6 36.6 %all-to-all-start.3 = ((bf16[16,384,128]{2,1,0:T(8,128)(2,1)}), bf16[16,384,128]{2,1,0:T(8,128)(2,1)S(1)}, u32[]{:S(2)}, u32[]{:S(2)}) async-start(bf16[16,384,128]{2,1,0:T(8,128)(2,1)} %owner_pieces.1), calls=%async_computation.3 | async-start | bytes 3145728 | tf_op jit(solution)/shard_map/all_to_all | solution.py:623
  129.5 2.0 %collective-permute-start.10 = (bf16[320,512]{1,0:T(8,128)(2,1)S(1)}, bf16[320,512]{1,0:T(8,128)(2,1)S(1)}, u32[]{:S(2)}, u32[]{:S(2)}) collective-permute-start(bf16[320,512]{1,0:T(8,128)(2,1)S(1)} %copy-done.13), channel_id=1, source_target_pairs={{0,1},{1,0},{2,3},{3,2},{4,5},{5,4},{6,7},{7,6},{8,9},{9,8},{10,11... | collective-permute-start | bytes 983048 | tf_op jit(solution)/shard_map/ppermute | solution.py:46
  141.4 21.6 %collective-permute-start.12 = (bf16[512,1024]{1,0:T(8,128)(2,1)}, bf16[512,1024]{1,0:T(8,128)(2,1)}, u32[]{:S(2)}, u32[]{:S(2)}) collective-permute-start(bf16[512,1024]{1,0:T(8,128)(2,1)} %collective-permute-done.7.refs_9_), channel_id=1, source_target_pairs={{0,6},{1,3},{2,0},{3,5},{4,2},{5,7},{6,4},{7,1},{8,14},{9,11},{10,... | collective-permute-start | bytes 3145736 | tf_op jit(solution)/shard_map/ppermute | solution.py:46
  143.1 3.8 %collective-permute-start.11 = (bf16[320,1024]{1,0:T(8,128)(2,1)}, bf16[320,1024]{1,0:T(8,128)(2,1)S(1)}, u32[]{:S(2)}, u32[]{:S(2)}) collective-permute-start(bf16[320,1024]{1,0:T(8,128)(2,1)} %get-tuple-element.97), channel_id=1, source_target_pairs={{0,1},{1,0},{2,3},{3,2},{4,5},{5,4},{6,7},{7,6},{8,9},{9,8},{10,11... | collective-permute-start | bytes 1966088 | tf_op jit(solution)/shard_map/ppermute | solution.py:46
  162.4 7.2 %collective-permute-start.14 = (bf16[320,2048]{1,0:T(8,128)(2,1)}, bf16[320,2048]{1,0:T(8,128)(2,1)S(1)}, u32[]{:S(2)}, u32[]{:S(2)}) collective-permute-start(bf16[320,2048]{1,0:T(8,128)(2,1)} %get-tuple-element.104), channel_id=1, source_target_pairs={{0,1},{1,0},{2,3},{3,2},{4,5},{5,4},{6,7},{7,6},{8,9},{9,8},{10,11... | collective-permute-start | bytes 3932168 | tf_op jit(solution)/shard_map/ppermute | solution.py:46
  162.8 6.8 %collective-permute-start.15 = (f32[320,1024]{1,0:T(8,128)}, f32[320,1024]{1,0:T(8,128)S(1)}, u32[]{:S(2)}, u32[]{:S(2)}) collective-permute-start(f32[320,1024]{1,0:T(8,128)} %get-tuple-element.106), channel_id=1, source_target_pairs={{0,1},{1,0},{2,3},{3,2},{4,5},{5,4},{6,7},{7,6},{8,9},{9,8},{10,11... | collective-permute-start | bytes 3932168 | tf_op jit(solution)/shard_map/ppermute | solution.py:46
  162.9 12.9 %collective-permute-start.13 = (bf16[512,1024]{1,0:T(8,128)(2,1)}, bf16[512,1024]{1,0:T(8,128)(2,1)}, u32[]{:S(2)}, u32[]{:S(2)}) collective-permute-start(bf16[512,1024]{1,0:T(8,128)(2,1)} %collective-permute-done.12.w_hbm), channel_id=1, source_target_pairs={{0,1},{1,0},{2,3},{3,2},{4,5},{5,4},{6,7},{7,6},{8,9},{9,8},{10,11... | collective-permute-start | bytes 3145736 | tf_op jit(solution)/shard_map/ppermute | solution.py:46
  163.3 19.5 %all-to-all-start.4 = ((bf16[8,192,256]{2,1,0:T(8,128)(2,1)}), bf16[8,192,256]{2,1,0:T(8,128)(2,1)S(1)}, u32[]{:S(2)}, u32[]{:S(2)}) async-start(bf16[8,192,256]{2,1,0:T(8,128)(2,1)} %sum_pieces.1), calls=%async_computation.4 | async-start | bytes 1572864 | tf_op jit(solution)/shard_map/all_to_all | solution.py:623
  (12 other events, 47.1 us)
Sparse Core Ops, SparseCore 0:
  10.4 90.6 all-gather.1

commit v3 on v2

--- a/solution.py
+++ b/solution.py
@@ -351,11 +351,13 @@
     )(place, master, prev_down, prior, prior_sib)
 
 
-def main_kernel(units, before, s_ref, t_hbm, tr_hbm, d_hbm, cot_hbm, br_hbm, *rest):
+def main_kernel(at, units, before, added, s_ref, t_hbm, tr_hbm, d_hbm, cot_hbm, br_hbm, *rest):
     n = t_hbm.shape[0]
     w_hbm, rest = rest[:units], rest[units:]
+    if added:
+        (v_hbm, _), rest = (rest[:2], rest[2]), rest[3:]
     if before:
-        (v_hbm, _, r_hbm), rest = rest[:3], rest[3:]
+        r_hbm, rest = rest[0], rest[1:]
     vo_hbm, vs_hbm, x_hbm, o_hbm, cot2, br, tbuf, wbuf, dbuf, xbuf, vbuf, lbuf, rest = *rest[:12], rest[12:]
     csems, tsems, wsems, osems, vsems, rsems = rest
 
@@ -370,14 +372,14 @@
         ins.append(
             [
                 pltpu.make_async_copy(w_hbm[u], wbuf.at[span(u)], wsems.at[0, u]),
-                pltpu.make_async_copy(d_hbm.at[column(s_ref[2 * units + before + u])], dbuf.at[u], wsems.at[1, u]),
+                pltpu.make_async_copy(d_hbm.at[column(s_ref[at + 2 * units + before + u])], dbuf.at[u], wsems.at[1, u]),
             ]
         )
-        here = t_hbm.at[:, column(s_ref[u])]
-        there = tr_hbm.at[:, column(s_ref[units + u])]
+        here = t_hbm.at[:, column(s_ref[at + u])]
+        there = tr_hbm.at[:, column(s_ref[at + units + u])]
         tokens.append(pltpu.make_async_copy(here, tbuf.at[pl.ds(0, n), span(u)], tsems.at[0, u]))
         tokens.append(pltpu.make_async_copy(there, tbuf.at[pl.ds(n, n), span(u)], tsems.at[1, u]))
-    if before:
+    if added:
         late.append(pltpu.make_async_copy(v_hbm[0], vbuf.at[pl.ds(0, n)], vsems.at[0, 4]))
         late.append(pltpu.make_async_copy(v_hbm[1], vbuf.at[pl.ds(n, n)], vsems.at[1, 4]))
     first = start(cot_copies(cot_hbm, tr_hbm, cot2, csems) + [pltpu.make_async_copy(br_hbm, br, csems.at[2])])
@@ -395,20 +397,20 @@
         xbuf[u] = x.astype(bf16)
         outs += start(
             [
-                pltpu.make_async_copy(xbuf.at[u, pl.ds(0, n)], x_hbm.at[:, column(s_ref[u])], osems.at[0, u]),
+                pltpu.make_async_copy(xbuf.at[u, pl.ds(0, n)], x_hbm.at[:, column(s_ref[at + u])], osems.at[0, u]),
                 pltpu.make_async_copy(xbuf.at[u, pl.ds(n, n)], o_hbm.at[:, span(u)], osems.at[1, u]),
             ]
         )
     wait(late)
     for u in range(before):
-        there = x_hbm.at[:, column(s_ref[2 * units + u])]
+        there = x_hbm.at[:, column(s_ref[at + 2 * units + u])]
         outs += start([pltpu.make_async_copy(lbuf.at[:, span(u)], there, rsems.at[u])])
     wait(tokens)
     for j in range(4):
         cols = slice(256 * j, 256 * j + 256)
         there = pl.ds(256 * j, 256)
         part = nn(tbuf[...], wbuf[:, cols])
-        vbuf[:, cols] = part + vbuf[:, cols] if before else part
+        vbuf[:, cols] = part + vbuf[:, cols] if added else part
         outs += start(
             [
                 pltpu.make_async_copy(vbuf.at[pl.ds(0, n), there], vo_hbm.at[:, there], vsems.at[0, j]),
@@ -418,23 +420,17 @@
     wait(outs)
 
 
-def main_group(tokens, tokens_sib, down, cot, br2, blocks, starts, before=0, carry=()):
+def main_group(table, at, tokens, tokens_sib, down, cot, br2, blocks, before=0, carry=()):
     n, d = tokens.shape
     units = len(blocks)
-    args = [starts, tokens, tokens_sib, down, cot, br2, *blocks]
-    kernel = main_kernel
+    args = [table, tokens, tokens_sib, down, cot, br2, *blocks]
     aliases = {}
-    if before:
+    if carry:
         aliases = {len(args) + 2: 2}
         args += list(carry)
 
-        def kernel(units, before, *refs):
-            at = 6 + units
-            refs = refs[:at] + ((refs[at], refs[at + 1]),) + refs[at + 2 :]
-            main_kernel(units, before, *refs)
-
     return call(
-        functools.partial(kernel, units, before),
+        functools.partial(main_kernel, at, units, before, bool(carry)),
         "main_group",
         args,
         [((n, 1024), f32), ((n, 1024), f32), ((n, d), bf16), ((n, 512 * units), bf16)],
@@ -510,14 +506,19 @@
     )(pieces)
 
 
-def place_kernel(s_ref, r_hbm, vo_hbm, vr_hbm, low_hbm, up_hbm, x_in, v_hbm, x_hbm, rbuf, vo, vr, low, up, sems, xsems, vsems):
+def place_kernel(at, s_ref, r_hbm, rs_hbm, vo_hbm, vr_hbm, low_hbm, up_hbm, x_in, v_hbm, x_hbm, rbuf, vo, vr, low, up, sems, xsems, vsems):
     ins = start([pltpu.make_async_copy(low_hbm, low, sems.at[0]), pltpu.make_async_copy(up_hbm, up, sems.at[1])])
-    late = start([pltpu.make_async_copy(r_hbm, rbuf, sems.at[2])])
+    late = start(
+        [
+            pltpu.make_async_copy(r_hbm, rbuf.at[:, pl.ds(0, 1024)], sems.at[2]),
+            pltpu.make_async_copy(rs_hbm, rbuf.at[:, pl.ds(1024, 2048)], sems.at[5]),
+        ]
+    )
     ins += start([pltpu.make_async_copy(vo_hbm, vo, sems.at[3]), pltpu.make_async_copy(vr_hbm, vr, sems.at[4])])
     wait(late)
     outs = []
-    for u in range(4):
-        there = x_hbm.at[:, column(s_ref[u])]
+    for u in range(6):
+        there = x_hbm.at[:, column(s_ref[at + u])]
         outs += start([pltpu.make_async_copy(rbuf.at[:, pl.ds(512 * u, 512)], there, xsems.at[u])])
     wait(ins)
     for j in range(4):
@@ -528,29 +529,29 @@
     wait(outs)
 
 
-def place_columns(x, recv, vo, vr, low, up, starts):
+def place_columns(table, at, x, recv, recv_last, vo, vr, low, up):
     n, d = x.shape
     return call(
-        place_kernel,
+        functools.partial(place_kernel, at),
         "place_columns",
-        (starts, recv, vo, vr, low, up, x),
+        (table, recv, recv_last, vo, vr, low, up, x),
         [((n, 1024), f32), ((n, d), bf16)],
         [
-            pltpu.VMEM((n, 2048), bf16),
+            pltpu.VMEM((n, 3072), bf16),
             pltpu.VMEM((n, 1024), f32),
             pltpu.VMEM((n, 1024), f32),
             pltpu.VMEM((n, 512), bf16),
             pltpu.VMEM((512, 1024), bf16),
-            pltpu.SemaphoreType.DMA((5,)),
-            pltpu.SemaphoreType.DMA((4,)),
+            pltpu.SemaphoreType.DMA((6,)),
+            pltpu.SemaphoreType.DMA((6,)),
             pltpu.SemaphoreType.DMA((4,)),
         ],
-        {6: 1},
+        {7: 1},
     )
 
 
 def finish_kernel(
-    s_ref, t_hbm, d_hbm, w_hbm, ws_hbm, cot_hbm, br_hbm, vs_hbm, x_in,
+    at, s_ref, t_hbm, d_hbm, w_hbm, ws_hbm, cot_hbm, br_hbm, vs_hbm, x_in,
     v_hbm, x_hbm, tbuf, wbuf, dbuf, xbuf, cot, br, vs, vbuf, sems, wsems, xsems, vsems,
 ):
     n = cot.shape[0]
@@ -566,20 +567,21 @@
         ins.append(
             [
                 pltpu.make_async_copy(w, wbuf.at[there], wsems.at[0, i]),
-                pltpu.make_async_copy(d_hbm.at[column(s_ref[i])], dbuf.at[i], wsems.at[1, i]),
+                pltpu.make_async_copy(d_hbm.at[column(s_ref[at + i])], dbuf.at[i], wsems.at[1, i]),
             ]
         )
-        rest.append(pltpu.make_async_copy(t_hbm.at[:, column(s_ref[i])], tbuf.at[:, there], wsems.at[2, i]))
+        rest.append(pltpu.make_async_copy(t_hbm.at[:, column(s_ref[at + i])], tbuf.at[:, there], wsems.at[2, i]))
     rest.append(pltpu.make_async_copy(vs_hbm, vs, sems.at[0]))
-    start(ins[0])
+    start(ins[0] + ins[1])
     wait(first)
     outs = []
     for i in range(2):
         wait(ins[i])
-        start(ins[1] if i == 0 else rest)
+        if i == 0:
+            start(rest)
         x = nt(cot[...], wbuf[512 * i : 512 * i + 512, :]) + scale * nt(br[...], dbuf[i])
         xbuf[i] = x.astype(bf16)
-        outs += start([pltpu.make_async_copy(xbuf.at[i], x_hbm.at[:, column(s_ref[i])], xsems.at[i])])
+        outs += start([pltpu.make_async_copy(xbuf.at[i], x_hbm.at[:, column(s_ref[at + i])], xsems.at[i])])
     wait(rest)
     for j in range(4):
         cols = slice(256 * j, 256 * j + 256)
@@ -589,12 +591,12 @@
     wait(outs)
 
 
-def finish(x, tokens, down, w, w_sib, cot, br2, vs, starts):
+def finish(table, at, x, tokens, down, w, w_sib, cot, br2, vs):
     n, d = x.shape
     return call(
-        finish_kernel,
+        functools.partial(finish_kernel, at),
         "finish",
-        (starts, tokens, down, w, w_sib, cot, br2, vs, x),
+        (table, tokens, down, w, w_sib, cot, br2, vs, x),
         [((n, 1024), bf16), ((n, d), bf16)],
         [
             pltpu.VMEM((n, 1024), bf16),
@@ -664,16 +666,13 @@
     own = groups_of(c)
     mine = [2 * k + c for k in own]
     sib = [2 * k + 1 - c for k in groups_of(1 - c)]
-    starts = [
-        jnp.concatenate([mine[0], own[0], 0 * own[0]]),
-        jnp.concatenate([mine[1], own[1], sib[0], mine[1]]),
-        jnp.concatenate([mine[2], own[2], sib[1], mine[2]]),
-        sib[2],
-        jnp.concatenate([mine[3], sib[3]]),
-    ]
-    starts = [v.astype(jnp.int32) for v in starts]
-
-    vo, vs, dx, other = main_group(tokens, tokens_sib, down_half, cot, br2, [w], starts[0])
+    parts = [mine[0], own[0], 0 * own[0]]
+    parts += [mine[1], own[1], mine[1]]
+    parts += [mine[2], own[2], sib[0], mine[2]]
+    parts += [sib[1], sib[2], mine[3], sib[3]]
+    table = jnp.concatenate(parts).astype(jnp.int32)
+
+    vo, vs, dx, other = main_group(table, 0, tokens, tokens_sib, down_half, cot, br2, [w])
     p, q, far, vo, vs, dx, other = bar(first + (vo, vs, dx, other))
     second = second_step(p, q, far)
 
@@ -681,19 +680,21 @@
     low = low_rank(tokens, down, place)
     pieces = owner_pieces(g, low, send(low, "core"), cot, tokens_sib, place)
     pieces, p = bar((pieces, p))
-    part = main_group(*shared, [p, q], starts[1], 1, (vo, vs, dx, send(other, "core")))
-    r, far_q, far_p, part = bar(second + (part,))
+    first_sib = send(other, "core")
+    part = main_group(table, 3, *shared, [p, q], 0, (vo, vs, dx))
+    r, far_q, far_p, part, first_sib = bar(second + (part, first_sib))
 
     far_r = send(far_q, "xq")
     pieces = to_owners(pieces, ("zh", "x", "zl"))
     vo, vs, dx, other = part
-    part = main_group(*shared, [far, r, far_p, far_q], starts[2], 2, (vo, vs, dx, send(other, "core")))
-    part, pieces = bar((part, sum_pieces(pieces)))
+    second_sib = send(other, "core")
+    part = main_group(table, 9, *shared, [far, r, far_p, far_q], 1, (vo, vs, dx, first_sib))
+    part, pieces, second_sib = bar((part, sum_pieces(pieces), second_sib))
 
     pieces = to_owners(pieces, ("y", "zl"))
     vo, vs, dx, other = part
-    v, dx = place_columns(dx, send(other, "core"), vo, send(vs, "core"), low, up_rows, starts[3])
-    values, dx = finish(dx, tokens, down, far_r, send(far_r, "core"), cot, br2, v, starts[4])
+    v, dx = place_columns(table, 22, dx, second_sib, send(other, "core"), vo, send(vs, "core"), low, up_rows)
+    values, dx = finish(table, 28, dx, tokens, down, far_r, send(far_r, "core"), cot, br2, v)
     pieces, values = bar((pieces, values))
     down_grad, up_grad = join_pieces(pieces)
     return merged, values, dx, down_grad, up_grad

time: 192 us -> 189 us (0.984)
  other arithmetic: 2.76 us -> 0.75 us
    ppermute x16, waiting for transfers between devices: 33.7 us -> 35.6 us  [send(): return lax.ppermute(v, AXES, MOVES[move])]
  transfers between devices with their start and end apart: 22 -> 22, of which waited for: 10 -> 9; matrix products, arithmetic and copies ran while one was open for 2% -> 1% of each run, Pallas kernels for 39% -> 39%
where the time goes in v3:
time: 189 us; the launch traced here: 188 us
  Pallas kernels  77.1 us (41%)
  waiting for transfers between devices  46.4 us (25%)
  starting transfers between devices  42.2 us (22%)
  between operations  14.3 us (8%)
  local copies, waits for them, and re-layouts  6.89 us (4%)
    pallas_call x9, Pallas kernels, call(): pl.pallas_call(kernel, in_specs=[pl.BlockSpec(memory_space=pltpu.SMEM)] +...  66.7 us
    ppermute x16, waiting for transfers between devices, send(): return lax.ppermute(v, AXES, MOVES[move])  35.6 us
    all_to_all x5, starting transfers between devices, to_owners(): return lax.all_to_all(v, axes, split_axis=0, concat_axis=0)  26.9 us
    ppermute x16, starting transfers between devices, send(): return lax.ppermute(v, AXES, MOVES[move])  15.3 us
    all_to_all x5, waiting for transfers between devices, to_owners(): return lax.all_to_all(v, axes, split_axis=0, concat_axis=0)  10.8 us
    pallas_call x1, Pallas kernels, merge(): pl.pallas_call(merge_kernel, grid=(1,), in_specs=[pl.BlockSpec(memory_spa...  5.84 us
    unnamed x28, local copies, waits for them, and re-layouts  5.05 us
  transfers between devices with their start and end apart: 22, of which 9 were waited for; matrix products, arithmetic and copies ran while one was open for 1% of the time, Pallas kernels for 39%

profile of v3, /device:TPU:1, one launch (start us, length us, event | category | flops | bytes accessed | tf_op | source)
XLA Modules:
  0.0 187.7 jit_solution(4476494772621993309)
XLA Ops:
  7.2 2.3 %prepare.1 = (bf16[8,32,1024]{2,1,0:T(8,128)(2,1)}, bf16[512,512]{1,0:T(8,128)(2,1)}) custom-call(f32[32,1024]{1,0:T(8,128)} %up_ref.1, f32[512,512]{1,0:T(8,128)} %down_ref.1), custom_call_target="tpu_custom_call" | custom-call | bytes 65536 | tf_op jit(solution)/shard_map/prepare/pallas_call | solution.py:118
  10.2 8.2 %all-to-all-start = ((bf16[8,32,1024]{2,1,0:T(8,128)(2,1)}), bf16[8,32,1024]{2,1,0:T(8,128)(2,1)S(1)}, u32[]{:S(2)}, u32[]{:S(2)}) async-start(bf16[8,32,1024]{2,1,0:T(8,128)(2,1)} %get-tuple-element.66), calls=%async_computation | async-start | bytes 1048576 | tf_op jit(solution)/shard_map/all_to_all | solution.py:625
  18.3 3.9 %pick_columns.1 = bf16[320,5120]{1,0:T(8,128)(2,1)} custom-call(s32[3]{0:T(128)} %pad_add_fusion.s_ref, bf16[320,8192]{1,0:T(8,128)(2,1)} %t_hbm.13, bf16[320,1024]{1,0:T(8,128)(2,1)} %cot_hbm.13), custom_call_target="tpu_custom_call" | custom-call | bytes 65536 | tf_op jit(solution)/shard_map/pick_columns/pallas_call | solution.py:63
  22.2 7.8 %all-to-all-done.up_hbm = bf16[8,32,1024]{2,1,0:T(8,128)(2,1)S(1)} async-done(((bf16[8,32,1024]{2,1,0:T(8,128)(2,1)}), bf16[8,32,1024]{2,1,0:T(8,128)(2,1)S(1)}, u32[]{:S(2)}, u32[]{:S(2)}) %all-to-all-start) | async-done | bytes 524320 | tf_op jit(solution)/shard_map/all_to_all | solution.py:625
  32.0 3.6 %all-to-all-start.1 = ((f32[8,32,1024]{2,1,0:T(8,128)}), f32[8,32,1024]{2,1,0:T(8,128)S(1)}, u32[]{:S(2)}, u32[]{:S(2)}) async-start(f32[8,32,1024]{2,1,0:T(8,128)} %broadcast_in_dim.4), calls=%async_computation.1 | async-start | bytes 2097152 | tf_op jit(solution)/shard_map/all_to_all | solution.py:625
  35.7 2.6 %collective-permute-done.1.ups_hbm = bf16[8,32,1024]{2,1,0:T(8,128)(2,1)S(1)} collective-permute-done((bf16[8,32,1024]{2,1,0:T(8,128)(2,1)S(1)}, bf16[8,32,1024]{2,1,0:T(8,128)(2,1)S(1)}, u32[]{:S(2)}, u32[]{:S(2)}) %collective-permute-start.1) | collective-permute-done | bytes 524320 | tf_op jit(solution)/shard_map/ppermute | solution.py:46
  39.0 10.9 %rank_partials.1 = (bf16[4,8,512,128]{3,2,1,0:T(8,128)(2,1)}, bf16[512,1024]{1,0:T(8,128)(2,1)}, bf16[640,512]{1,0:T(8,128)(2,1)}) custom-call(s32[3]{0:T(128)} %pad_add_fusion.s_ref, bf16[320,8192]{1,0:T(8,128)(2,1)} %t_hbm.13, bf16[320,5120]{1,0:T(8,128)(2,1)} %collective-permute-done.tr_hbm, bf16[320,1024]{1,0:T(8,128)(2,1)} %cot_hbm.13, ...), custom_call_target="tpu_custom_call" | custom-call | bytes 65536 | tf_op jit(solution)/shard_map/rank_partials/pallas_call | solution.py:63
  50.0 3.0 %all-to-all-done.1.b_ref = f32[8,32,1024]{2,1,0:T(8,128)S(1)} async-done(((f32[8,32,1024]{2,1,0:T(8,128)}), f32[8,32,1024]{2,1,0:T(8,128)S(1)}, u32[]{:S(2)}, u32[]{:S(2)}) %all-to-all-start.1) | async-done | bytes 1048608 | tf_op jit(solution)/shard_map/all_to_all | solution.py:625
  53.0 5.3 %all-to-all-start.2 = ((bf16[4,8,512,128]{3,2,1,0:T(8,128)(2,1)}), bf16[4,8,512,128]{3,2,1,0:T(8,128)(2,1)}, u32[]{:S(2)}, u32[]{:S(2)}) async-start(bf16[4,8,512,128]{3,2,1,0:T(8,128)(2,1)} %get-tuple-element.82), calls=%async_computation.2 | async-start | bytes 8388608 | tf_op jit(solution)/shard_map/all_to_all | solution.py:625
  58.9 2.3 %collective-permute-done.2.bs_ref = f32[8,32,1024]{2,1,0:T(8,128)S(1)} collective-permute-done((f32[8,32,1024]{2,1,0:T(8,128)S(1)}, f32[8,32,1024]{2,1,0:T(8,128)S(1)}, u32[]{:S(2)}, u32[]{:S(2)}) %collective-permute-start.2) | collective-permute-done | bytes 1048608 | tf_op jit(solution)/shard_map/ppermute | solution.py:46
  62.5 5.8 %merge.1 = (f32[512,1024]{1,0:T(8,128)}, bf16[512,1024]{1,0:T(8,128)(2,1)}) custom-call(s32[3]{0:T(128)S(1)} %copy-done.2, f32[512,1024]{1,0:T(8,128)S(1)} %copy-done, f32[512,512]{1,0:T(8,128)S(1)} %copy-done.1, f32[8,32,1024]{2,1,0:T(8,128)S(1)} %all-to-all-done.1.b_ref, f32[8,32,1024]{2,1,0:T(8,128)S(1)} %collective-permute-done.2.bs_ref), custom_call_target="tpu_custom_call" | custom-call | bytes 65536 | tf_op jit(solution)/shard_map/merge/pallas_call | solution.py:335
  68.3 2.1 %collective-permute-start.5 = (bf16[512,1024]{1,0:T(8,128)(2,1)}, bf16[512,1024]{1,0:T(8,128)(2,1)S(1)}, u32[]{:S(2)}, u32[]{:S(2)}) collective-permute-start(bf16[512,1024]{1,0:T(8,128)(2,1)} %get-tuple-element.75.rest_0_), channel_id=1, source_target_pairs={{0,24},{1,25},{2,26},{3,27},{4,28},{5,29},{6,30},{7,31},{8,16},{9,... | collective-permute-start | bytes 3145736 | tf_op jit(solution)/shard_map/ppermute | solution.py:46
  73.9 6.0 %main_group.3 = (f32[320,1024]{1,0:T(8,128)}, f32[320,1024]{1,0:T(8,128)}, bf16[320,8192]{1,0:T(8,128)(2,1)}, bf16[320,512]{1,0:T(8,128)(2,1)}) custom-call(s32[30]{0:T(128)} %concatenate.4.s_ref, bf16[320,8192]{1,0:T(8,128)(2,1)} %t_hbm.13, bf16[320,5120]{1,0:T(8,128)(2,1)} %collective-permute-done.tr_hbm, bf16[512,512]{1,0:T(8,128)(2,1)} %get-tuple-element.73.d_hbm, ...), custom_call_target="tpu_custom_call" | custom-call | bytes 65536 | tf_op jit(solution)/shard_map/main_group/pallas_call | solution.py:63
  79.9 23.8 %collective-permute-done.5.rest_0_ = bf16[512,1024]{1,0:T(8,128)(2,1)S(1)} collective-permute-done((bf16[512,1024]{1,0:T(8,128)(2,1)}, bf16[512,1024]{1,0:T(8,128)(2,1)S(1)}, u32[]{:S(2)}, u32[]{:S(2)}) %collective-permute-start.5) | collective-permute-done | bytes 1048608 | tf_op jit(solution)/shard_map/ppermute | solution.py:46
  108.7 6.9 %low_rank.1.low_hbm = bf16[320,512]{1,0:T(8,128)(2,1)} custom-call(s32[3]{0:T(128)} %pad_add_fusion.s_ref, bf16[320,8192]{1,0:T(8,128)(2,1)} %t_hbm.13, bf16[8192,512]{1,0:T(8,128)(2,1)} %all-gather.2.cloned.1.call-done.d_hbm), custom_call_target="tpu_custom_call" | custom-call | bytes 65536 | tf_op jit(solution)/shard_map/low_rank/pallas_call | solution.py:63
  119.0 5.7 %owner_pieces.1 = bf16[16,384,128]{2,1,0:T(8,128)(2,1)} custom-call(s32[3]{0:T(128)} %pad_add_fusion.s_ref, bf16[4,8,512,128]{3,2,1,0:T(8,128)(2,1)} %all-to-all-done.2.g_hbm, bf16[320,512]{1,0:T(8,128)(2,1)} %low_rank.1.low_hbm, bf16[320,512]{1,0:T(8,128)(2,1)} %copy-done.11, bf16[320,1024]{1,0:T(8,128)(2,1)} %cot_hbm.13, ...), custom_call_target="tpu_custom_call" | custom-call | bytes 65536 | tf_op jit(solution)/shard_map/owner_pieces/pallas_call | solution.py:63
  124.7 5.1 %all-to-all-start.3 = ((bf16[16,384,128]{2,1,0:T(8,128)(2,1)}), bf16[16,384,128]{2,1,0:T(8,128)(2,1)S(1)}, u32[]{:S(2)}, u32[]{:S(2)}) async-start(bf16[16,384,128]{2,1,0:T(8,128)(2,1)} %owner_pieces.1), calls=%async_computation.3 | async-start | bytes 3145728 | tf_op jit(solution)/shard_map/all_to_all | solution.py:625
  130.5 9.0 %main_group.4 = (f32[320,1024]{1,0:T(8,128)}, f32[320,1024]{1,0:T(8,128)}, bf16[320,8192]{1,0:T(8,128)(2,1)}, bf16[320,1024]{1,0:T(8,128)(2,1)}) custom-call(s32[30]{0:T(128)} %concatenate.4.s_ref, bf16[320,8192]{1,0:T(8,128)(2,1)} %t_hbm.13, bf16[320,5120]{1,0:T(8,128)(2,1)} %collective-permute-done.tr_hbm, ...), custom_call_target="tpu_custom_call", output_to_operand_aliasing={{2}: (10, {})} | custom-call | bytes 65536 | tf_op jit(solution)/shard_map/main_group/pallas_call | solution.py:63
  139.6 1.7 collective-permute-start.12
  142.8 13.4 %main_group.5 = (f32[320,1024]{1,0:T(8,128)}, f32[320,1024]{1,0:T(8,128)}, bf16[320,8192]{1,0:T(8,128)(2,1)}, bf16[320,2048]{1,0:T(8,128)(2,1)}) custom-call(s32[30]{0:T(128)} %concatenate.4.s_ref, bf16[320,8192]{1,0:T(8,128)(2,1)} %t_hbm.13, bf16[320,5120]{1,0:T(8,128)(2,1)} %collective-permute-done.tr_hbm, ...), custom_call_target="tpu_custom_call", output_to_operand_aliasing={{2}: (12, {})} | custom-call | bytes 65536 | tf_op jit(solution)/shard_map/main_group/pallas_call | solution.py:63
  158.7 3.8 %collective-permute-done.12.w_hbm = bf16[512,1024]{1,0:T(8,128)(2,1)} collective-permute-done((bf16[512,1024]{1,0:T(8,128)(2,1)}, bf16[512,1024]{1,0:T(8,128)(2,1)}, u32[]{:S(2)}, u32[]{:S(2)}) %collective-permute-start.12) | collective-permute-done | bytes 1048608 | tf_op jit(solution)/shard_map/ppermute | solution.py:46
  162.6 4.8 %all-to-all-start.4 = ((bf16[8,192,256]{2,1,0:T(8,128)(2,1)}), bf16[8,192,256]{2,1,0:T(8,128)(2,1)S(1)}, u32[]{:S(2)}, u32[]{:S(2)}) async-start(bf16[8,192,256]{2,1,0:T(8,128)(2,1)} %sum_pieces.1), calls=%async_computation.4 | async-start | bytes 1572864 | tf_op jit(solution)/shard_map/all_to_all | solution.py:625
  168.8 5.0 %place_columns.1 = (f32[320,1024]{1,0:T(8,128)}, bf16[320,8192]{1,0:T(8,128)(2,1)}) custom-call(s32[30]{0:T(128)} %concatenate.4.s_ref, bf16[320,1024]{1,0:T(8,128)(2,1)} %copy-done.8, bf16[320,2048]{1,0:T(8,128)(2,1)} %copy-done.4, f32[320,1024]{1,0:T(8,128)} %get-tuple-element.109.vo_hbm, f32[320,1024]{1,0:T(8,128)} %copy-done.5, ...), custom_call_target="tpu_custom_call", output_to_operand_aliasing={{1}: (7, {})} | custom-call | bytes 65536 | tf_op jit(solution)/shard_map/place_columns/pallas_call | solution.py:63
  173.9 5.9 %finish.1 = (bf16[320,1024]{1,0:T(8,128)(2,1)}, bf16[320,8192]{1,0:T(8,128)(2,1)}) custom-call(s32[30]{0:T(128)} %concatenate.4.s_ref, bf16[320,8192]{1,0:T(8,128)(2,1)} %t_hbm.13, bf16[8192,512]{1,0:T(8,128)(2,1)} %all-gather.2.cloned.1.call-done.d_hbm, bf16[512,1024]{1,0:T(8,128)(2,1)} %collective-permute-done.12.w_hbm, ...), custom_call_target="tpu_custom_call", output_to_operand_aliasing={{1}: (8, {})} | custom-call | bytes 65536 | tf_op jit(solution)/shard_map/finish/pallas_call | solution.py:63
  (67 shorter events, 24.5 us)
Async XLA Ops:
  7.2 101.5 %all-gather.2.cloned.1.call-start = ((), (), s32[]{:S(2)}) async-start(), calls=%async_computation.5 | async-start | bytes 8912896 | tf_op jit(solution)/shard_map/all_gather | solution.py:642
  10.2 19.9 %all-to-all-start = ((bf16[8,32,1024]{2,1,0:T(8,128)(2,1)}), bf16[8,32,1024]{2,1,0:T(8,128)(2,1)S(1)}, u32[]{:S(2)}, u32[]{:S(2)}) async-start(bf16[8,32,1024]{2,1,0:T(8,128)(2,1)} %get-tuple-element.66), calls=%async_computation | async-start | bytes 1048576 | tf_op jit(solution)/shard_map/all_to_all | solution.py:625
  18.3 11.7 %copy-start.12 = (f32[32,1024]{1,0:T(8,128)S(1)}, f32[32,1024]{1,0:T(8,128)}, u32[]{:S(2)}) copy-start(f32[32,1024]{1,0:T(8,128)} %param.10) | copy-start | bytes 393220
  31.2 7.1 %collective-permute-start = (bf16[320,5120]{1,0:T(8,128)(2,1)}, bf16[320,5120]{1,0:T(8,128)(2,1)}, u32[]{:S(2)}, u32[]{:S(2)}) collective-permute-start(bf16[320,5120]{1,0:T(8,128)(2,1)} %pick_columns.1), channel_id=1, source_target_pairs={{0,1},{1,0},{2,3},{3,2},{4,5},{5,4},{6,7},{7,6},{8,9},{9,8},{10,11... | collective-permute-start | bytes 9830408 | tf_op jit(solution)/shard_map/ppermute | solution.py:46
  32.0 21.0 %all-to-all-start.1 = ((f32[8,32,1024]{2,1,0:T(8,128)}), f32[8,32,1024]{2,1,0:T(8,128)S(1)}, u32[]{:S(2)}, u32[]{:S(2)}) async-start(f32[8,32,1024]{2,1,0:T(8,128)} %broadcast_in_dim.4), calls=%async_computation.1 | async-start | bytes 2097152 | tf_op jit(solution)/shard_map/all_to_all | solution.py:625
  35.6 2.7 %collective-permute-start.1 = (bf16[8,32,1024]{2,1,0:T(8,128)(2,1)S(1)}, bf16[8,32,1024]{2,1,0:T(8,128)(2,1)S(1)}, u32[]{:S(2)}, u32[]{:S(2)}) collective-permute-start(bf16[8,32,1024]{2,1,0:T(8,128)(2,1)S(1)} %all-to-all-done.up_hbm), channel_id=1, source_target_pairs={{0,1},{1,0},{2,3},{3,2},{4,5},{5,4},{6,7},{7,6},{8,9},{9,8},{10,11... | collective-permute-start | bytes 1572872 | tf_op jit(solution)/shard_map/ppermute | solution.py:46
  53.0 63.8 %all-to-all-start.2 = ((bf16[4,8,512,128]{3,2,1,0:T(8,128)(2,1)}), bf16[4,8,512,128]{3,2,1,0:T(8,128)(2,1)}, u32[]{:S(2)}, u32[]{:S(2)}) async-start(bf16[4,8,512,128]{3,2,1,0:T(8,128)(2,1)} %get-tuple-element.82), calls=%async_computation.2 | async-start | bytes 8388608 | tf_op jit(solution)/shard_map/all_to_all | solution.py:625
  58.3 3.0 %collective-permute-start.2 = (f32[8,32,1024]{2,1,0:T(8,128)S(1)}, f32[8,32,1024]{2,1,0:T(8,128)S(1)}, u32[]{:S(2)}, u32[]{:S(2)}) collective-permute-start(f32[8,32,1024]{2,1,0:T(8,128)S(1)} %all-to-all-done.1.b_ref), channel_id=1, source_target_pairs={{0,1},{1,0},{2,3},{3,2},{4,5},{5,4},{6,7},{7,6},{8,9},{9,8},{10,11... | collective-permute-start | bytes 3145736 | tf_op jit(solution)/shard_map/ppermute | solution.py:46
  68.3 35.5 %collective-permute-start.5 = (bf16[512,1024]{1,0:T(8,128)(2,1)}, bf16[512,1024]{1,0:T(8,128)(2,1)S(1)}, u32[]{:S(2)}, u32[]{:S(2)}) collective-permute-start(bf16[512,1024]{1,0:T(8,128)(2,1)} %get-tuple-element.75.rest_0_), channel_id=1, source_target_pairs={{0,24},{1,25},{2,26},{3,27},{4,28},{5,29},{6,30},{7,31},{8,16},{9,... | collective-permute-start | bytes 3145736 | tf_op jit(solution)/shard_map/ppermute | solution.py:46
  70.4 34.2 %collective-permute-start.4 = (bf16[512,1024]{1,0:T(8,128)(2,1)}, bf16[512,1024]{1,0:T(8,128)(2,1)S(1)}, u32[]{:S(2)}, u32[]{:S(2)}) collective-permute-start(bf16[512,1024]{1,0:T(8,128)(2,1)} %get-tuple-element.75.rest_0_), channel_id=1, source_target_pairs={{0,6},{1,3},{2,0},{3,5},{4,2},{5,7},{6,4},{7,1},{8,14},{9,11},{10,... | collective-permute-start | bytes 3145736 | tf_op jit(solution)/shard_map/ppermute | solution.py:46
  71.5 33.9 %collective-permute-start.3 = (bf16[512,1024]{1,0:T(8,128)(2,1)}, bf16[512,1024]{1,0:T(8,128)(2,1)}, u32[]{:S(2)}, u32[]{:S(2)}) collective-permute-start(bf16[512,1024]{1,0:T(8,128)(2,1)} %get-tuple-element.75.rest_0_), channel_id=1, source_target_pairs={{0,2},{1,7},{2,4},{3,1},{4,6},{5,3},{6,0},{7,5},{8,10},{9,15},{10,... | collective-permute-start | bytes 3145736 | tf_op jit(solution)/shard_map/ppermute | solution.py:46
  103.8 11.9 %copy-start.6 = (bf16[512,1024]{1,0:T(8,128)(2,1)}, bf16[512,1024]{1,0:T(8,128)(2,1)S(1)}, u32[]{:S(2)}) copy-start(bf16[512,1024]{1,0:T(8,128)(2,1)S(1)} %collective-permute-done.5.rest_0_) | copy-start | bytes 3145732
  105.4 34.2 %collective-permute-start.7 = (bf16[512,1024]{1,0:T(8,128)(2,1)S(1)}, bf16[512,1024]{1,0:T(8,128)(2,1)}, u32[]{:S(2)}, u32[]{:S(2)}) collective-permute-start(bf16[512,1024]{1,0:T(8,128)(2,1)S(1)} %collective-permute-done.5.rest_0_), channel_id=1, source_target_pairs={{0,6},{1,3},{2,0},{3,5},{4,2},{5,7},{6,4},{7,1},{8,14},{9,11},{10,... | collective-permute-start | bytes 3145736 | tf_op jit(solution)/shard_map/ppermute | solution.py:46
  105.8 33.8 %collective-permute-start.8 = (bf16[512,1024]{1,0:T(8,128)(2,1)}, bf16[512,1024]{1,0:T(8,128)(2,1)}, u32[]{:S(2)}, u32[]{:S(2)}) collective-permute-start(bf16[512,1024]{1,0:T(8,128)(2,1)} %collective-permute-done.3.rest_0_), channel_id=1, source_target_pairs={{0,24},{1,25},{2,26},{3,27},{4,28},{5,29},{6,30},{7,31},{8,16},{9,... | collective-permute-start | bytes 3145736 | tf_op jit(solution)/shard_map/ppermute | solution.py:46
  107.2 32.3 %collective-permute-start.6 = (bf16[512,1024]{1,0:T(8,128)(2,1)}, bf16[512,1024]{1,0:T(8,128)(2,1)}, u32[]{:S(2)}, u32[]{:S(2)}) collective-permute-start(bf16[512,1024]{1,0:T(8,128)(2,1)} %collective-permute-done.3.rest_0_), channel_id=1, source_target_pairs={{0,2},{1,7},{2,4},{3,1},{4,6},{5,3},{6,0},{7,5},{8,10},{9,15},{10,... | collective-permute-start | bytes 3145736 | tf_op jit(solution)/shard_map/ppermute | solution.py:46
  115.7 2.6 %collective-permute-start.9 = (bf16[320,512]{1,0:T(8,128)(2,1)}, bf16[320,512]{1,0:T(8,128)(2,1)S(1)}, u32[]{:S(2)}, u32[]{:S(2)}) collective-permute-start(bf16[320,512]{1,0:T(8,128)(2,1)} %low_rank.1.low_hbm), channel_id=1, source_target_pairs={{0,1},{1,0},{2,3},{3,2},{4,5},{5,4},{6,7},{7,6},{8,9},{9,8},{10,11... | collective-permute-start | bytes 983048 | tf_op jit(solution)/shard_map/ppermute | solution.py:46
  124.7 31.5 %all-to-all-start.3 = ((bf16[16,384,128]{2,1,0:T(8,128)(2,1)}), bf16[16,384,128]{2,1,0:T(8,128)(2,1)S(1)}, u32[]{:S(2)}, u32[]{:S(2)}) async-start(bf16[16,384,128]{2,1,0:T(8,128)(2,1)} %owner_pieces.1), calls=%async_computation.3 | async-start | bytes 3145728 | tf_op jit(solution)/shard_map/all_to_all | solution.py:625
  129.8 9.7 %collective-permute-start.10 = (bf16[320,512]{1,0:T(8,128)(2,1)S(1)}, bf16[320,512]{1,0:T(8,128)(2,1)S(1)}, u32[]{:S(2)}, u32[]{:S(2)}) collective-permute-start(bf16[320,512]{1,0:T(8,128)(2,1)S(1)} %copy-done.13), channel_id=1, source_target_pairs={{0,1},{1,0},{2,3},{3,2},{4,5},{5,4},{6,7},{7,6},{8,9},{9,8},{10,11... | collective-permute-start | bytes 983048 | tf_op jit(solution)/shard_map/ppermute | solution.py:46
  139.6 23.0 %collective-permute-start.12 = (bf16[512,1024]{1,0:T(8,128)(2,1)}, bf16[512,1024]{1,0:T(8,128)(2,1)}, u32[]{:S(2)}, u32[]{:S(2)}) collective-permute-start(bf16[512,1024]{1,0:T(8,128)(2,1)} %collective-permute-done.7.rest_3_), channel_id=1, source_target_pairs={{0,6},{1,3},{2,0},{3,5},{4,2},{5,7},{6,4},{7,1},{8,14},{9,11},{10,... | collective-permute-start | bytes 3145736 | tf_op jit(solution)/shard_map/ppermute | solution.py:46
  141.3 16.1 %collective-permute-start.11 = (bf16[320,1024]{1,0:T(8,128)(2,1)}, bf16[320,1024]{1,0:T(8,128)(2,1)S(1)}, u32[]{:S(2)}, u32[]{:S(2)}) collective-permute-start(bf16[320,1024]{1,0:T(8,128)(2,1)} %get-tuple-element.105), channel_id=1, source_target_pairs={{0,1},{1,0},{2,3},{3,2},{4,5},{5,4},{6,7},{7,6},{8,9},{9,8},{10,11... | collective-permute-start | bytes 1966088 | tf_op jit(solution)/shard_map/ppermute | solution.py:46
  158.2 9.1 %collective-permute-start.14 = (bf16[320,2048]{1,0:T(8,128)(2,1)}, bf16[320,2048]{1,0:T(8,128)(2,1)S(1)}, u32[]{:S(2)}, u32[]{:S(2)}) collective-permute-start(bf16[320,2048]{1,0:T(8,128)(2,1)} %get-tuple-element.108), channel_id=1, source_target_pairs={{0,1},{1,0},{2,3},{3,2},{4,5},{5,4},{6,7},{7,6},{8,9},{9,8},{10,11... | collective-permute-start | bytes 3932168 | tf_op jit(solution)/shard_map/ppermute | solution.py:46
  158.2 9.1 %collective-permute-start.15 = (f32[320,1024]{1,0:T(8,128)}, f32[320,1024]{1,0:T(8,128)S(1)}, u32[]{:S(2)}, u32[]{:S(2)}) collective-permute-start(f32[320,1024]{1,0:T(8,128)} %get-tuple-element.110), channel_id=1, source_target_pairs={{0,1},{1,0},{2,3},{3,2},{4,5},{5,4},{6,7},{7,6},{8,9},{9,8},{10,11... | collective-permute-start | bytes 3932168 | tf_op jit(solution)/shard_map/ppermute | solution.py:46
  162.6 11.3 %collective-permute-start.13 = (bf16[512,1024]{1,0:T(8,128)(2,1)}, bf16[512,1024]{1,0:T(8,128)(2,1)}, u32[]{:S(2)}, u32[]{:S(2)}) collective-permute-start(bf16[512,1024]{1,0:T(8,128)(2,1)} %collective-permute-done.12.w_hbm), channel_id=1, source_target_pairs={{0,1},{1,0},{2,3},{3,2},{4,5},{5,4},{6,7},{7,6},{8,9},{9,8},{10,11... | collective-permute-start | bytes 3145736 | tf_op jit(solution)/shard_map/ppermute | solution.py:46
  162.6 17.2 %all-to-all-start.4 = ((bf16[8,192,256]{2,1,0:T(8,128)(2,1)}), bf16[8,192,256]{2,1,0:T(8,128)(2,1)S(1)}, u32[]{:S(2)}, u32[]{:S(2)}) async-start(bf16[8,192,256]{2,1,0:T(8,128)(2,1)} %sum_pieces.1), calls=%async_computation.4 | async-start | bytes 1572864 | tf_op jit(solution)/shard_map/all_to_all | solution.py:625
  (12 other events, 50.3 us)
Sparse Core Ops, SparseCore 0:
  10.4 90.8 all-gather.1

commit v4 on v3

--- a/solution.py
+++ b/solution.py
@@ -383,14 +383,15 @@
         late.append(pltpu.make_async_copy(v_hbm[0], vbuf.at[pl.ds(0, n)], vsems.at[0, 4]))
         late.append(pltpu.make_async_copy(v_hbm[1], vbuf.at[pl.ds(n, n)], vsems.at[1, 4]))
     first = start(cot_copies(cot_hbm, tr_hbm, cot2, csems) + [pltpu.make_async_copy(br_hbm, br, csems.at[2])])
-    start(ins[0])
+    for u in range(min(units, 2)):
+        start(ins[u])
     wait(first)
     outs = []
     for u in range(units):
         wait(ins[u])
-        if u + 1 < units:
-            start(ins[u + 1])
-        else:
+        if u + 2 < units:
+            start(ins[u + 2])
+        if u == 0:
             start(late)
         start(tokens[2 * u : 2 * u + 2])
         x = nt(cot2[...], wbuf[512 * u : 512 * u + 512, :]) + scale * nt(br[...], dbuf[u])

time: 189 us -> 189 us (level)
  no operation moved by 1% of the time
where the time goes in v4:
time: 189 us; the launch traced here: 188 us
  Pallas kernels  75.8 us (40%)
  waiting for transfers between devices  47.6 us (25%)
  starting transfers between devices  42.4 us (22%)
  between operations  14.3 us (8%)
  local copies, waits for them, and re-layouts  6.89 us (4%)
    pallas_call x9, Pallas kernels, call(): pl.pallas_call(kernel, in_specs=[pl.BlockSpec(memory_space=pltpu.SMEM)] +...  65.4 us
    ppermute x16, waiting for transfers between devices, send(): return lax.ppermute(v, AXES, MOVES[move])  36.7 us
    all_to_all x5, starting transfers between devices, to_owners(): return lax.all_to_all(v, axes, split_axis=0, concat_axis=0)  26.9 us
    ppermute x16, starting transfers between devices, send(): return lax.ppermute(v, AXES, MOVES[move])  15.4 us
    all_to_all x5, waiting for transfers between devices, to_owners(): return lax.all_to_all(v, axes, split_axis=0, concat_axis=0)  10.8 us
    pallas_call x1, Pallas kernels, merge(): pl.pallas_call(merge_kernel, grid=(1,), in_specs=[pl.BlockSpec(memory_spa...  5.84 us
    unnamed x28, local copies, waits for them, and re-layouts  5.05 us
  transfers between devices with their start and end apart: 22, of which 9 were waited for; matrix products, arithmetic and copies ran while one was open for 1% of the time, Pallas kernels for 39%

profile of v4, /device:TPU:1, one launch (start us, length us, event | category | flops | bytes accessed | tf_op | source)
XLA Modules:
  0.0 187.7 jit_solution(1689067405047063622)
XLA Ops:
  7.2 2.3 %prepare.1 = (bf16[8,32,1024]{2,1,0:T(8,128)(2,1)}, bf16[512,512]{1,0:T(8,128)(2,1)}) custom-call(f32[32,1024]{1,0:T(8,128)} %up_ref.1, f32[512,512]{1,0:T(8,128)} %down_ref.1), custom_call_target="tpu_custom_call" | custom-call | bytes 65536 | tf_op jit(solution)/shard_map/prepare/pallas_call | solution.py:118
  10.2 8.2 %all-to-all-start = ((bf16[8,32,1024]{2,1,0:T(8,128)(2,1)}), bf16[8,32,1024]{2,1,0:T(8,128)(2,1)S(1)}, u32[]{:S(2)}, u32[]{:S(2)}) async-start(bf16[8,32,1024]{2,1,0:T(8,128)(2,1)} %get-tuple-element.66), calls=%async_computation | async-start | bytes 1048576 | tf_op jit(solution)/shard_map/all_to_all | solution.py:626
  18.3 3.9 %pick_columns.1 = bf16[320,5120]{1,0:T(8,128)(2,1)} custom-call(s32[3]{0:T(128)} %pad_add_fusion.s_ref, bf16[320,8192]{1,0:T(8,128)(2,1)} %t_hbm.13, bf16[320,1024]{1,0:T(8,128)(2,1)} %cot_hbm.13), custom_call_target="tpu_custom_call" | custom-call | bytes 65536 | tf_op jit(solution)/shard_map/pick_columns/pallas_call | solution.py:63
  22.2 7.8 %all-to-all-done.up_hbm = bf16[8,32,1024]{2,1,0:T(8,128)(2,1)S(1)} async-done(((bf16[8,32,1024]{2,1,0:T(8,128)(2,1)}), bf16[8,32,1024]{2,1,0:T(8,128)(2,1)S(1)}, u32[]{:S(2)}, u32[]{:S(2)}) %all-to-all-start) | async-done | bytes 524320 | tf_op jit(solution)/shard_map/all_to_all | solution.py:626
  32.0 3.6 %all-to-all-start.1 = ((f32[8,32,1024]{2,1,0:T(8,128)}), f32[8,32,1024]{2,1,0:T(8,128)S(1)}, u32[]{:S(2)}, u32[]{:S(2)}) async-start(f32[8,32,1024]{2,1,0:T(8,128)} %broadcast_in_dim.4), calls=%async_computation.1 | async-start | bytes 2097152 | tf_op jit(solution)/shard_map/all_to_all | solution.py:626
  35.7 2.6 %collective-permute-done.1.ups_hbm = bf16[8,32,1024]{2,1,0:T(8,128)(2,1)S(1)} collective-permute-done((bf16[8,32,1024]{2,1,0:T(8,128)(2,1)S(1)}, bf16[8,32,1024]{2,1,0:T(8,128)(2,1)S(1)}, u32[]{:S(2)}, u32[]{:S(2)}) %collective-permute-start.1) | collective-permute-done | bytes 524320 | tf_op jit(solution)/shard_map/ppermute | solution.py:46
  39.0 10.9 %rank_partials.1 = (bf16[4,8,512,128]{3,2,1,0:T(8,128)(2,1)}, bf16[512,1024]{1,0:T(8,128)(2,1)}, bf16[640,512]{1,0:T(8,128)(2,1)}) custom-call(s32[3]{0:T(128)} %pad_add_fusion.s_ref, bf16[320,8192]{1,0:T(8,128)(2,1)} %t_hbm.13, bf16[320,5120]{1,0:T(8,128)(2,1)} %collective-permute-done.tr_hbm, bf16[320,1024]{1,0:T(8,128)(2,1)} %cot_hbm.13, ...), custom_call_target="tpu_custom_call" | custom-call | bytes 65536 | tf_op jit(solution)/shard_map/rank_partials/pallas_call | solution.py:63
  50.0 3.0 %all-to-all-done.1.b_ref = f32[8,32,1024]{2,1,0:T(8,128)S(1)} async-done(((f32[8,32,1024]{2,1,0:T(8,128)}), f32[8,32,1024]{2,1,0:T(8,128)S(1)}, u32[]{:S(2)}, u32[]{:S(2)}) %all-to-all-start.1) | async-done | bytes 1048608 | tf_op jit(solution)/shard_map/all_to_all | solution.py:626
  53.0 5.3 %all-to-all-start.2 = ((bf16[4,8,512,128]{3,2,1,0:T(8,128)(2,1)}), bf16[4,8,512,128]{3,2,1,0:T(8,128)(2,1)}, u32[]{:S(2)}, u32[]{:S(2)}) async-start(bf16[4,8,512,128]{3,2,1,0:T(8,128)(2,1)} %get-tuple-element.82), calls=%async_computation.2 | async-start | bytes 8388608 | tf_op jit(solution)/shard_map/all_to_all | solution.py:626
  58.9 2.3 %collective-permute-done.2.bs_ref = f32[8,32,1024]{2,1,0:T(8,128)S(1)} collective-permute-done((f32[8,32,1024]{2,1,0:T(8,128)S(1)}, f32[8,32,1024]{2,1,0:T(8,128)S(1)}, u32[]{:S(2)}, u32[]{:S(2)}) %collective-permute-start.2) | collective-permute-done | bytes 1048608 | tf_op jit(solution)/shard_map/ppermute | solution.py:46
  62.5 5.8 %merge.1 = (f32[512,1024]{1,0:T(8,128)}, bf16[512,1024]{1,0:T(8,128)(2,1)}) custom-call(s32[3]{0:T(128)S(1)} %copy-done.2, f32[512,1024]{1,0:T(8,128)S(1)} %copy-done, f32[512,512]{1,0:T(8,128)S(1)} %copy-done.1, f32[8,32,1024]{2,1,0:T(8,128)S(1)} %all-to-all-done.1.b_ref, f32[8,32,1024]{2,1,0:T(8,128)S(1)} %collective-permute-done.2.bs_ref), custom_call_target="tpu_custom_call" | custom-call | bytes 65536 | tf_op jit(solution)/shard_map/merge/pallas_call | solution.py:335
  68.3 2.1 %collective-permute-start.5 = (bf16[512,1024]{1,0:T(8,128)(2,1)}, bf16[512,1024]{1,0:T(8,128)(2,1)S(1)}, u32[]{:S(2)}, u32[]{:S(2)}) collective-permute-start(bf16[512,1024]{1,0:T(8,128)(2,1)} %get-tuple-element.75.rest_0_), channel_id=1, source_target_pairs={{0,24},{1,25},{2,26},{3,27},{4,28},{5,29},{6,30},{7,31},{8,16},{9,... | collective-permute-start | bytes 3145736 | tf_op jit(solution)/shard_map/ppermute | solution.py:46
  73.9 6.0 %main_group.3 = (f32[320,1024]{1,0:T(8,128)}, f32[320,1024]{1,0:T(8,128)}, bf16[320,8192]{1,0:T(8,128)(2,1)}, bf16[320,512]{1,0:T(8,128)(2,1)}) custom-call(s32[30]{0:T(128)} %concatenate.4.s_ref, bf16[320,8192]{1,0:T(8,128)(2,1)} %t_hbm.13, bf16[320,5120]{1,0:T(8,128)(2,1)} %collective-permute-done.tr_hbm, bf16[512,512]{1,0:T(8,128)(2,1)} %get-tuple-element.73.d_hbm, ...), custom_call_target="tpu_custom_call" | custom-call | bytes 65536 | tf_op jit(solution)/shard_map/main_group/pallas_call | solution.py:63
  79.9 23.8 %collective-permute-done.5.rest_0_ = bf16[512,1024]{1,0:T(8,128)(2,1)S(1)} collective-permute-done((bf16[512,1024]{1,0:T(8,128)(2,1)}, bf16[512,1024]{1,0:T(8,128)(2,1)S(1)}, u32[]{:S(2)}, u32[]{:S(2)}) %collective-permute-start.5) | collective-permute-done | bytes 1048608 | tf_op jit(solution)/shard_map/ppermute | solution.py:46
  108.7 6.9 %low_rank.1.low_hbm = bf16[320,512]{1,0:T(8,128)(2,1)} custom-call(s32[3]{0:T(128)} %pad_add_fusion.s_ref, bf16[320,8192]{1,0:T(8,128)(2,1)} %t_hbm.13, bf16[8192,512]{1,0:T(8,128)(2,1)} %all-gather.2.cloned.1.call-done.d_hbm), custom_call_target="tpu_custom_call" | custom-call | bytes 65536 | tf_op jit(solution)/shard_map/low_rank/pallas_call | solution.py:63
  119.0 5.7 %owner_pieces.1 = bf16[16,384,128]{2,1,0:T(8,128)(2,1)} custom-call(s32[3]{0:T(128)} %pad_add_fusion.s_ref, bf16[4,8,512,128]{3,2,1,0:T(8,128)(2,1)} %all-to-all-done.2.g_hbm, bf16[320,512]{1,0:T(8,128)(2,1)} %low_rank.1.low_hbm, bf16[320,512]{1,0:T(8,128)(2,1)} %copy-done.11, bf16[320,1024]{1,0:T(8,128)(2,1)} %cot_hbm.13, ...), custom_call_target="tpu_custom_call" | custom-call | bytes 65536 | tf_op jit(solution)/shard_map/owner_pieces/pallas_call | solution.py:63
  124.7 5.1 %all-to-all-start.3 = ((bf16[16,384,128]{2,1,0:T(8,128)(2,1)}), bf16[16,384,128]{2,1,0:T(8,128)(2,1)S(1)}, u32[]{:S(2)}, u32[]{:S(2)}) async-start(bf16[16,384,128]{2,1,0:T(8,128)(2,1)} %owner_pieces.1), calls=%async_computation.3 | async-start | bytes 3145728 | tf_op jit(solution)/shard_map/all_to_all | solution.py:626
  130.5 8.7 %main_group.4 = (f32[320,1024]{1,0:T(8,128)}, f32[320,1024]{1,0:T(8,128)}, bf16[320,8192]{1,0:T(8,128)(2,1)}, bf16[320,1024]{1,0:T(8,128)(2,1)}) custom-call(s32[30]{0:T(128)} %concatenate.4.s_ref, bf16[320,8192]{1,0:T(8,128)(2,1)} %t_hbm.13, bf16[320,5120]{1,0:T(8,128)(2,1)} %collective-permute-done.tr_hbm, ...), custom_call_target="tpu_custom_call", output_to_operand_aliasing={{2}: (10, {})} | custom-call | bytes 65536 | tf_op jit(solution)/shard_map/main_group/pallas_call | solution.py:63
  139.3 1.7 collective-permute-start.12
  142.5 12.4 %main_group.5 = (f32[320,1024]{1,0:T(8,128)}, f32[320,1024]{1,0:T(8,128)}, bf16[320,8192]{1,0:T(8,128)(2,1)}, bf16[320,2048]{1,0:T(8,128)(2,1)}) custom-call(s32[30]{0:T(128)} %concatenate.4.s_ref, bf16[320,8192]{1,0:T(8,128)(2,1)} %t_hbm.13, bf16[320,5120]{1,0:T(8,128)(2,1)} %collective-permute-done.tr_hbm, ...), custom_call_target="tpu_custom_call", output_to_operand_aliasing={{2}: (12, {})} | custom-call | bytes 65536 | tf_op jit(solution)/shard_map/main_group/pallas_call | solution.py:63
  157.6 5.0 %collective-permute-done.12.w_hbm = bf16[512,1024]{1,0:T(8,128)(2,1)} collective-permute-done((bf16[512,1024]{1,0:T(8,128)(2,1)}, bf16[512,1024]{1,0:T(8,128)(2,1)}, u32[]{:S(2)}, u32[]{:S(2)}) %collective-permute-start.12) | collective-permute-done | bytes 1048608 | tf_op jit(solution)/shard_map/ppermute | solution.py:46
  162.6 4.8 %all-to-all-start.4 = ((bf16[8,192,256]{2,1,0:T(8,128)(2,1)}), bf16[8,192,256]{2,1,0:T(8,128)(2,1)S(1)}, u32[]{:S(2)}, u32[]{:S(2)}) async-start(bf16[8,192,256]{2,1,0:T(8,128)(2,1)} %sum_pieces.1), calls=%async_computation.4 | async-start | bytes 1572864 | tf_op jit(solution)/shard_map/all_to_all | solution.py:626
  168.8 5.0 %place_columns.1 = (f32[320,1024]{1,0:T(8,128)}, bf16[320,8192]{1,0:T(8,128)(2,1)}) custom-call(s32[30]{0:T(128)} %concatenate.4.s_ref, bf16[320,1024]{1,0:T(8,128)(2,1)} %copy-done.8, bf16[320,2048]{1,0:T(8,128)(2,1)} %copy-done.4, f32[320,1024]{1,0:T(8,128)} %get-tuple-element.109.vo_hbm, f32[320,1024]{1,0:T(8,128)} %copy-done.5, ...), custom_call_target="tpu_custom_call", output_to_operand_aliasing={{1}: (7, {})} | custom-call | bytes 65536 | tf_op jit(solution)/shard_map/place_columns/pallas_call | solution.py:63
  173.9 5.9 %finish.1 = (bf16[320,1024]{1,0:T(8,128)(2,1)}, bf16[320,8192]{1,0:T(8,128)(2,1)}) custom-call(s32[30]{0:T(128)} %concatenate.4.s_ref, bf16[320,8192]{1,0:T(8,128)(2,1)} %t_hbm.13, bf16[8192,512]{1,0:T(8,128)(2,1)} %all-gather.2.cloned.1.call-done.d_hbm, bf16[512,1024]{1,0:T(8,128)(2,1)} %collective-permute-done.12.w_hbm, ...), custom_call_target="tpu_custom_call", output_to_operand_aliasing={{1}: (8, {})} | custom-call | bytes 65536 | tf_op jit(solution)/shard_map/finish/pallas_call | solution.py:63
  (67 shorter events, 24.7 us)
Async XLA Ops:
  7.2 101.5 %all-gather.2.cloned.1.call-start = ((), (), s32[]{:S(2)}) async-start(), calls=%async_computation.5 | async-start | bytes 8912896 | tf_op jit(solution)/shard_map/all_gather | solution.py:643
  10.2 19.9 %all-to-all-start = ((bf16[8,32,1024]{2,1,0:T(8,128)(2,1)}), bf16[8,32,1024]{2,1,0:T(8,128)(2,1)S(1)}, u32[]{:S(2)}, u32[]{:S(2)}) async-start(bf16[8,32,1024]{2,1,0:T(8,128)(2,1)} %get-tuple-element.66), calls=%async_computation | async-start | bytes 1048576 | tf_op jit(solution)/shard_map/all_to_all | solution.py:626
  18.3 11.7 %copy-start.12 = (f32[32,1024]{1,0:T(8,128)S(1)}, f32[32,1024]{1,0:T(8,128)}, u32[]{:S(2)}) copy-start(f32[32,1024]{1,0:T(8,128)} %param.10) | copy-start | bytes 393220
  31.2 7.1 %collective-permute-start = (bf16[320,5120]{1,0:T(8,128)(2,1)}, bf16[320,5120]{1,0:T(8,128)(2,1)}, u32[]{:S(2)}, u32[]{:S(2)}) collective-permute-start(bf16[320,5120]{1,0:T(8,128)(2,1)} %pick_columns.1), channel_id=1, source_target_pairs={{0,1},{1,0},{2,3},{3,2},{4,5},{5,4},{6,7},{7,6},{8,9},{9,8},{10,11... | collective-permute-start | bytes 9830408 | tf_op jit(solution)/shard_map/ppermute | solution.py:46
  32.0 21.0 %all-to-all-start.1 = ((f32[8,32,1024]{2,1,0:T(8,128)}), f32[8,32,1024]{2,1,0:T(8,128)S(1)}, u32[]{:S(2)}, u32[]{:S(2)}) async-start(f32[8,32,1024]{2,1,0:T(8,128)} %broadcast_in_dim.4), calls=%async_computation.1 | async-start | bytes 2097152 | tf_op jit(solution)/shard_map/all_to_all | solution.py:626
  35.6 2.7 %collective-permute-start.1 = (bf16[8,32,1024]{2,1,0:T(8,128)(2,1)S(1)}, bf16[8,32,1024]{2,1,0:T(8,128)(2,1)S(1)}, u32[]{:S(2)}, u32[]{:S(2)}) collective-permute-start(bf16[8,32,1024]{2,1,0:T(8,128)(2,1)S(1)} %all-to-all-done.up_hbm), channel_id=1, source_target_pairs={{0,1},{1,0},{2,3},{3,2},{4,5},{5,4},{6,7},{7,6},{8,9},{9,8},{10,11... | collective-permute-start | bytes 1572872 | tf_op jit(solution)/shard_map/ppermute | solution.py:46
  53.0 63.8 %all-to-all-start.2 = ((bf16[4,8,512,128]{3,2,1,0:T(8,128)(2,1)}), bf16[4,8,512,128]{3,2,1,0:T(8,128)(2,1)}, u32[]{:S(2)}, u32[]{:S(2)}) async-start(bf16[4,8,512,128]{3,2,1,0:T(8,128)(2,1)} %get-tuple-element.82), calls=%async_computation.2 | async-start | bytes 8388608 | tf_op jit(solution)/shard_map/all_to_all | solution.py:626
  58.3 3.0 %collective-permute-start.2 = (f32[8,32,1024]{2,1,0:T(8,128)S(1)}, f32[8,32,1024]{2,1,0:T(8,128)S(1)}, u32[]{:S(2)}, u32[]{:S(2)}) collective-permute-start(f32[8,32,1024]{2,1,0:T(8,128)S(1)} %all-to-all-done.1.b_ref), channel_id=1, source_target_pairs={{0,1},{1,0},{2,3},{3,2},{4,5},{5,4},{6,7},{7,6},{8,9},{9,8},{10,11... | collective-permute-start | bytes 3145736 | tf_op jit(solution)/shard_map/ppermute | solution.py:46
  68.3 35.5 %collective-permute-start.5 = (bf16[512,1024]{1,0:T(8,128)(2,1)}, bf16[512,1024]{1,0:T(8,128)(2,1)S(1)}, u32[]{:S(2)}, u32[]{:S(2)}) collective-permute-start(bf16[512,1024]{1,0:T(8,128)(2,1)} %get-tuple-element.75.rest_0_), channel_id=1, source_target_pairs={{0,24},{1,25},{2,26},{3,27},{4,28},{5,29},{6,30},{7,31},{8,16},{9,... | collective-permute-start | bytes 3145736 | tf_op jit(solution)/shard_map/ppermute | solution.py:46
  70.4 34.2 %collective-permute-start.4 = (bf16[512,1024]{1,0:T(8,128)(2,1)}, bf16[512,1024]{1,0:T(8,128)(2,1)S(1)}, u32[]{:S(2)}, u32[]{:S(2)}) collective-permute-start(bf16[512,1024]{1,0:T(8,128)(2,1)} %get-tuple-element.75.rest_0_), channel_id=1, source_target_pairs={{0,6},{1,3},{2,0},{3,5},{4,2},{5,7},{6,4},{7,1},{8,14},{9,11},{10,... | collective-permute-start | bytes 3145736 | tf_op jit(solution)/shard_map/ppermute | solution.py:46
  71.5 33.9 %collective-permute-start.3 = (bf16[512,1024]{1,0:T(8,128)(2,1)}, bf16[512,1024]{1,0:T(8,128)(2,1)}, u32[]{:S(2)}, u32[]{:S(2)}) collective-permute-start(bf16[512,1024]{1,0:T(8,128)(2,1)} %get-tuple-element.75.rest_0_), channel_id=1, source_target_pairs={{0,2},{1,7},{2,4},{3,1},{4,6},{5,3},{6,0},{7,5},{8,10},{9,15},{10,... | collective-permute-start | bytes 3145736 | tf_op jit(solution)/shard_map/ppermute | solution.py:46
  103.8 11.9 %copy-start.6 = (bf16[512,1024]{1,0:T(8,128)(2,1)}, bf16[512,1024]{1,0:T(8,128)(2,1)S(1)}, u32[]{:S(2)}) copy-start(bf16[512,1024]{1,0:T(8,128)(2,1)S(1)} %collective-permute-done.5.rest_0_) | copy-start | bytes 3145732
  105.4 33.9 %collective-permute-start.7 = (bf16[512,1024]{1,0:T(8,128)(2,1)S(1)}, bf16[512,1024]{1,0:T(8,128)(2,1)}, u32[]{:S(2)}, u32[]{:S(2)}) collective-permute-start(bf16[512,1024]{1,0:T(8,128)(2,1)S(1)} %collective-permute-done.5.rest_0_), channel_id=1, source_target_pairs={{0,6},{1,3},{2,0},{3,5},{4,2},{5,7},{6,4},{7,1},{8,14},{9,11},{10,... | collective-permute-start | bytes 3145736 | tf_op jit(solution)/shard_map/ppermute | solution.py:46
  105.8 33.5 %collective-permute-start.8 = (bf16[512,1024]{1,0:T(8,128)(2,1)}, bf16[512,1024]{1,0:T(8,128)(2,1)}, u32[]{:S(2)}, u32[]{:S(2)}) collective-permute-start(bf16[512,1024]{1,0:T(8,128)(2,1)} %collective-permute-done.3.rest_0_), channel_id=1, source_target_pairs={{0,24},{1,25},{2,26},{3,27},{4,28},{5,29},{6,30},{7,31},{8,16},{9,... | collective-permute-start | bytes 3145736 | tf_op jit(solution)/shard_map/ppermute | solution.py:46
  107.2 32.0 %collective-permute-start.6 = (bf16[512,1024]{1,0:T(8,128)(2,1)}, bf16[512,1024]{1,0:T(8,128)(2,1)}, u32[]{:S(2)}, u32[]{:S(2)}) collective-permute-start(bf16[512,1024]{1,0:T(8,128)(2,1)} %collective-permute-done.3.rest_0_), channel_id=1, source_target_pairs={{0,2},{1,7},{2,4},{3,1},{4,6},{5,3},{6,0},{7,5},{8,10},{9,15},{10,... | collective-permute-start | bytes 3145736 | tf_op jit(solution)/shard_map/ppermute | solution.py:46
  115.7 2.6 %collective-permute-start.9 = (bf16[320,512]{1,0:T(8,128)(2,1)}, bf16[320,512]{1,0:T(8,128)(2,1)S(1)}, u32[]{:S(2)}, u32[]{:S(2)}) collective-permute-start(bf16[320,512]{1,0:T(8,128)(2,1)} %low_rank.1.low_hbm), channel_id=1, source_target_pairs={{0,1},{1,0},{2,3},{3,2},{4,5},{5,4},{6,7},{7,6},{8,9},{9,8},{10,11... | collective-permute-start | bytes 983048 | tf_op jit(solution)/shard_map/ppermute | solution.py:46
  124.7 30.2 %all-to-all-start.3 = ((bf16[16,384,128]{2,1,0:T(8,128)(2,1)}), bf16[16,384,128]{2,1,0:T(8,128)(2,1)S(1)}, u32[]{:S(2)}, u32[]{:S(2)}) async-start(bf16[16,384,128]{2,1,0:T(8,128)(2,1)} %owner_pieces.1), calls=%async_computation.3 | async-start | bytes 3145728 | tf_op jit(solution)/shard_map/all_to_all | solution.py:626
  129.8 9.4 %collective-permute-start.10 = (bf16[320,512]{1,0:T(8,128)(2,1)S(1)}, bf16[320,512]{1,0:T(8,128)(2,1)S(1)}, u32[]{:S(2)}, u32[]{:S(2)}) collective-permute-start(bf16[320,512]{1,0:T(8,128)(2,1)S(1)} %copy-done.13), channel_id=1, source_target_pairs={{0,1},{1,0},{2,3},{3,2},{4,5},{5,4},{6,7},{7,6},{8,9},{9,8},{10,11... | collective-permute-start | bytes 983048 | tf_op jit(solution)/shard_map/ppermute | solution.py:46
  139.3 23.3 %collective-permute-start.12 = (bf16[512,1024]{1,0:T(8,128)(2,1)}, bf16[512,1024]{1,0:T(8,128)(2,1)}, u32[]{:S(2)}, u32[]{:S(2)}) collective-permute-start(bf16[512,1024]{1,0:T(8,128)(2,1)} %collective-permute-done.7.rest_3_), channel_id=1, source_target_pairs={{0,6},{1,3},{2,0},{3,5},{4,2},{5,7},{6,4},{7,1},{8,14},{9,11},{10,... | collective-permute-start | bytes 3145736 | tf_op jit(solution)/shard_map/ppermute | solution.py:46
  141.0 15.1 %collective-permute-start.11 = (bf16[320,1024]{1,0:T(8,128)(2,1)}, bf16[320,1024]{1,0:T(8,128)(2,1)S(1)}, u32[]{:S(2)}, u32[]{:S(2)}) collective-permute-start(bf16[320,1024]{1,0:T(8,128)(2,1)} %get-tuple-element.105), channel_id=1, source_target_pairs={{0,1},{1,0},{2,3},{3,2},{4,5},{5,4},{6,7},{7,6},{8,9},{9,8},{10,11... | collective-permute-start | bytes 1966088 | tf_op jit(solution)/shard_map/ppermute | solution.py:46
  156.9 10.4 %collective-permute-start.14 = (bf16[320,2048]{1,0:T(8,128)(2,1)}, bf16[320,2048]{1,0:T(8,128)(2,1)S(1)}, u32[]{:S(2)}, u32[]{:S(2)}) collective-permute-start(bf16[320,2048]{1,0:T(8,128)(2,1)} %get-tuple-element.108), channel_id=1, source_target_pairs={{0,1},{1,0},{2,3},{3,2},{4,5},{5,4},{6,7},{7,6},{8,9},{9,8},{10,11... | collective-permute-start | bytes 3932168 | tf_op jit(solution)/shard_map/ppermute | solution.py:46
  157.6 9.8 %collective-permute-start.15 = (f32[320,1024]{1,0:T(8,128)}, f32[320,1024]{1,0:T(8,128)S(1)}, u32[]{:S(2)}, u32[]{:S(2)}) collective-permute-start(f32[320,1024]{1,0:T(8,128)} %get-tuple-element.110), channel_id=1, source_target_pairs={{0,1},{1,0},{2,3},{3,2},{4,5},{5,4},{6,7},{7,6},{8,9},{9,8},{10,11... | collective-permute-start | bytes 3932168 | tf_op jit(solution)/shard_map/ppermute | solution.py:46
  162.6 11.3 %collective-permute-start.13 = (bf16[512,1024]{1,0:T(8,128)(2,1)}, bf16[512,1024]{1,0:T(8,128)(2,1)}, u32[]{:S(2)}, u32[]{:S(2)}) collective-permute-start(bf16[512,1024]{1,0:T(8,128)(2,1)} %collective-permute-done.12.w_hbm), channel_id=1, source_target_pairs={{0,1},{1,0},{2,3},{3,2},{4,5},{5,4},{6,7},{7,6},{8,9},{9,8},{10,11... | collective-permute-start | bytes 3145736 | tf_op jit(solution)/shard_map/ppermute | solution.py:46
  162.6 17.2 %all-to-all-start.4 = ((bf16[8,192,256]{2,1,0:T(8,128)(2,1)}), bf16[8,192,256]{2,1,0:T(8,128)(2,1)S(1)}, u32[]{:S(2)}, u32[]{:S(2)}) async-start(bf16[8,192,256]{2,1,0:T(8,128)(2,1)} %sum_pieces.1), calls=%async_computation.4 | async-start | bytes 1572864 | tf_op jit(solution)/shard_map/all_to_all | solution.py:626
  (12 other events, 50.3 us)
Sparse Core Ops, SparseCore 0:
  10.4 90.8 all-gather.1
